TPU v7x, 32 devices: a whole 2x2x4 slice. The times are simulated.
32 devices in a mesh: visit: 4 (over y, x), patch: 8 (over z, core).
Axes of the slice: x: 2, y: 2, z: 4, core: 2. Of those that a mesh axis runs over, the one named last changes fastest.
Arguments:
- pixels: bfloat16 [2048, 128, 128], P(('visit', 'patch')), may hold values from -6 to 6
- mask_bits: int32 [2048, 128, 128], P(('visit', 'patch')), may hold values from 0 to 15, as said below
- inv_var: float32 [2048], P(('visit', 'patch')), may hold values from 0.05 to 1
- owner: int32 [2048], P(('visit', 'patch')), may hold values from 0 to 7, as said below
- cell: int32 [2048], P(('visit', 'patch')), may hold values from 0 to 63
- coef_index: int32 [2048], P(('visit', 'patch')), may hold values from 0 to 63
- coef_table: float32 [64, 9], replicated, may hold values from -4 to 4
Outputs:
- coadd: float32 [512, 128, 128], P('patch', 'visit')
- difference: bfloat16 [2048, 128, 128], P(('visit', 'patch'))
Inputs may be any that keep to these rules, and one draw needn't show every extreme that they name: `owner`: within each device's 64 blocks (aligned runs of 64 in order) no patch is named more than 32 times; one patch, the same for all devices, is named exactly 32 times in every such run. `mask_bits`: each value is a sum of the bit flags 1, 2, 4 and 8.
All inputs are finite; a program needn't handle non-finite values.
Results may differ from a plain program's by a relative error of at most 0.0071.
Values may be sent and summed in bfloat16 or wider, within the bound.
A program may use at most 128 MiB of HBM per device.

v0:
```python
import jax
import jax.numpy as jnp
from jax import lax
from jax.sharding import PartitionSpec as P

CELLS = 64
KSIZE = 21


gauss_widths = (1.0, 2.0, 3.5)


def band_tables(side_len):
    tap_reach = KSIZE // 2
    position = jnp.arange(side_len).astype(jnp.float32)
    offset = position[:, None] - position[None, :]
    inside = jnp.abs(offset) <= tap_reach
    tap_offsets = jnp.arange(-tap_reach, tap_reach + 1).astype(jnp.float32)
    tables = []
    for spread in gauss_widths:
        profile_sum = jnp.sum(jnp.exp(-tap_offsets * tap_offsets / (2.0 * spread * spread)))
        even_band = jnp.where(
            inside, jnp.exp(-offset * offset / (2.0 * spread * spread)) / profile_sum, 0.0
        )
        tables.append(even_band)
        tables.append(even_band * offset / spread)
    return jnp.stack(tables)


def match_group(blocks, coefficients, tables, right_bands):
    number = blocks.shape[0]
    side_len = blocks.shape[1]
    columns = jnp.dot(
        blocks.reshape(number * side_len, side_len), right_bands, preferred_element_type=jnp.float32
    )
    columns = columns.astype(jnp.bfloat16).reshape(number, side_len, 6, side_len)
    left_parts = []
    for sigma_pos in range(3):
        even_band = tables[2 * sigma_pos]
        odd_band = tables[2 * sigma_pos + 1]
        left_parts.append(
            coefficients[:, 3 * sigma_pos, None, None] * even_band
            + coefficients[:, 3 * sigma_pos + 1, None, None] * odd_band
        )
        left_parts.append(coefficients[:, 3 * sigma_pos + 2, None, None] * even_band)
    left_bands = jnp.stack(left_parts, axis=2).astype(jnp.bfloat16)
    result = jnp.einsum("nisp,npsj->nij", left_bands, columns, preferred_element_type=jnp.float32)
    return result.astype(jnp.bfloat16)


def match_blocks(blocks, coefficients, tables, right_bands):
    number = blocks.shape[0]
    side_len = blocks.shape[1]
    batch_blocks = 16
    rounds = -(-number // batch_blocks)

    def one_batch(bundle):
        return match_group(bundle[0], bundle[1], tables, right_bands)

    matched = lax.map(
        one_batch,
        (
            blocks.reshape(rounds, batch_blocks, side_len, side_len),
            coefficients.reshape(rounds, batch_blocks, coefficients.shape[1]),
        ),
    )
    return matched.reshape(rounds * batch_blocks, side_len, side_len)[:number]


def shards(pixels, mask_bits, inv_var, owner, cell, coef_index, coef_table):
    blocks_here = pixels.shape[0]
    side_len = pixels.shape[1]
    kernel_sets = coef_table.shape[0]
    patches = lax.axis_size("patch")
    visits = lax.axis_size("visit")
    capacity = 4 * blocks_here // patches
    slot_total = patches * capacity
    tables = band_tables(side_len)
    right_bands = (
        jnp.transpose(tables, (2, 0, 1)).reshape(side_len, 6 * side_len).astype(jnp.bfloat16)
    )
    usable = (mask_bits % 2 == 0) & (mask_bits // 2 % 2 == 0) & (mask_bits // 4 % 2 == 0)
    masked = jnp.where(usable, pixels, jnp.zeros((), jnp.bfloat16))
    weight = inv_var.astype(jnp.bfloat16)
    cell_weight = jnp.where(
        cell[:, None] == jnp.arange(CELLS)[None, :], weight[:, None], jnp.zeros((), jnp.bfloat16)
    )
    chosen = (coef_index[:, None] == jnp.arange(kernel_sets)[None, :]).astype(jnp.bfloat16)
    dest_onehot = (owner[:, None] == jnp.arange(patches)[None, :]).astype(jnp.int32)
    slot_rank = jnp.sum((jnp.cumsum(dest_onehot, axis=0) - dest_onehot) * dest_onehot, axis=1)
    slot_of_block = owner * capacity + slot_rank
    matches = slot_of_block[None, :] == jnp.arange(slot_total)[:, None]
    source_row = jnp.sum(jnp.where(matches, jnp.arange(blocks_here)[None, :], 0), axis=1)
    filled = jnp.any(matches, axis=1)

    def pack_slots(values):
        picked = values[source_row]
        keep_rows = filled.reshape((slot_total,) + (1,) * (values.ndim - 1))
        picked = jnp.where(keep_rows, picked, jnp.zeros((), values.dtype))
        return picked.reshape((patches, capacity) + values.shape[1:])

    pieces = lax.all_to_all(pack_slots(masked), "patch", split_axis=0, concat_axis=0, tiled=True)
    weights = lax.all_to_all(
        pack_slots(cell_weight), "patch", split_axis=0, concat_axis=0, tiled=True
    )
    kernel_picks = lax.all_to_all(
        pack_slots(chosen), "patch", split_axis=0, concat_axis=0, tiled=True
    )
    flat_blocks = pieces.reshape((-1, side_len, side_len))
    coefficients = jnp.dot(
        kernel_picks.reshape(-1, kernel_sets).astype(jnp.float32),
        coef_table,
        precision=lax.Precision.HIGHEST,
    )
    matched = match_blocks(flat_blocks, coefficients, tables, right_bands)
    matched_slots = matched.reshape(pieces.shape)
    flat_weights = weights.reshape(slot_total, CELLS)
    flat_matched = matched_slots.reshape(slot_total, side_len * side_len)
    numerator = jnp.einsum(
        "sc,sk->ck", flat_weights, flat_matched, preferred_element_type=jnp.float32
    ).reshape(CELLS, side_len, side_len)
    weight_sum = jnp.sum(flat_weights.astype(jnp.float32), axis=0)
    rows_here = side_len // visits
    numerator, weight_sum = lax.psum((numerator, weight_sum), "visit")
    coadd_full = numerator / jnp.maximum(weight_sum, 1.0)[:, None, None]
    coadd_part = lax.dynamic_slice_in_dim(
        coadd_full, lax.axis_index("visit") * rows_here, rows_here, 1
    )
    template = coadd_full.astype(jnp.bfloat16)
    live_slots = (flat_weights > 0).astype(jnp.bfloat16)
    slot_template = jnp.einsum(
        "sc,ck->sk",
        live_slots,
        template.reshape(CELLS, side_len * side_len),
        preferred_element_type=jnp.float32,
    )
    difference_slots = (flat_matched.astype(jnp.float32) - slot_template).astype(jnp.bfloat16)
    returned = lax.all_to_all(
        difference_slots.reshape(patches, capacity, side_len, side_len),
        "patch",
        split_axis=0,
        concat_axis=0,
        tiled=True,
    )
    difference = returned.reshape(slot_total, side_len, side_len)[slot_of_block]
    return (coadd_part, difference)


def solution(mesh):
    placed = (
        P(("visit", "patch"), None, None),
        P(("visit", "patch"), None, None),
        P(("visit", "patch")),
        P(("visit", "patch")),
        P(("visit", "patch")),
        P(("visit", "patch")),
        P(),
    )
    return jax.shard_map(
        shards,
        mesh=mesh,
        in_specs=placed,
        out_specs=(P("patch", "visit", None), P(("visit", "patch"), None, None)),
        check_vma=False,
    )
```

profile of v0, /device:TPU:0, one launch (start us, length us, event | category | flops | bytes accessed | tf_op | source)
XLA Modules:
  0.0 868.2 jit_solution(6926169351445092044)
XLA Ops:
  14.5 6.3 all-to-all-start.1
  20.8 10.6 %fusion.62 = bf16[64,128,128]{2,1,0:T(8,128)(2,1)S(1)} fusion(bf16[64,128,128]{2,1,0:T(8,128)(2,1)} %param.9, s32[64,128,128]{2,1,0:T(8,128)} %param.10), kind=kLoop, calls=%fused_computation.94 | loop fusion | flops 59768832 | bytes 8388608 | tf_op jit(solution)/shard_map/jit(_where)/select_n | solution.py:83
  31.5 8.4 gather_fusion.2
  40.6 5.1 all-to-all-start
  45.7 7.2 broadcast_select_fusion
  52.9 5.1 all-to-all-start.2
  58.0 11.7 %all-reduce.2.cloned.1.call-start = ((), (), s32[]{:S(2)}) async-start(), calls=%async_computation.4 | async-start | bytes 8388608 | tf_op jit(solution)/shard_map/psum | solution.py:124
  77.1 165.0 %all-to-all-done.2 = bf16[8,32,128,128]{3,2,1,0:T(8,128)(2,1)} async-done(((bf16[8,32,128,128]{3,2,1,0:T(8,128)(2,1)}), bf16[8,32,128,128]{3,2,1,0:T(8,128)(2,1)}, u32[]{:S(2)}, u32[]{:S(2)}) %all-to-all-start.2) | async-done | bytes 8388640 | tf_op jit(solution)/shard_map/all_to_all | solution.py:102
  242.0 252.1 %while.12 = (s32[]{:T(128)}, bf16[16,16,128,128]{3,2,1,0:T(8,128)(2,1)}, f32[16,16,9]{1,2,0:T(8,128)S(1)}, bf16[16,16,128,128]{3,2,1,0:T(8,128)(2,1)}, bf16[128,...) while((s32[]{:T(128)}, ...), condition=%wide.region_8.9_spmd.clone.clone, body=%wide.region_7.8_spmd.clone.clone.sunk | while | flops 812171264 | bytes 35789844 | solution.py:60
  268.6 4.9 fusion.126
  284.4 4.9 fusion.126
  300.2 4.9 fusion.126
  315.9 4.9 fusion.126
  331.7 4.9 fusion.126
  363.2 4.9 fusion.126
  394.7 4.9 fusion.126
  410.5 4.9 fusion.126
  426.2 4.9 fusion.126
  442.0 4.9 fusion.126
  457.7 4.9 fusion.126
  489.2 4.9 fusion.126
  494.2 23.1 %copy.58 = bf16[32,8,128,128]{3,1,2,0:T(8,128)(2,1)} copy(bf16[32,8,128,128]{3,2,1,0:T(8,128)(2,1)} %bitcast.111) | data formatting | bytes 16777216
  517.3 11.9 %copy.34 = bf16[16384,256]{1,0:T(8,128)(2,1)} copy(bf16[16384,256]{0,1:T(8,128)(2,1)} %bitcast.116) | data formatting | bytes 16777216 | tf_op jit(solution)/shard_map/sc,sk->ck/dot_general | solution.py:119
  529.2 8.0 fusion.95
  537.3 10.3 %psum.15 = f32[64]{0:T(128)S(1)} all-reduce(f32[64]{0:T(128)S(1)} %convert_reduce_fusion), channel_id=1, replica_groups=mesh['visit'=4,'patch'=8] {'visit'}, use_global_device_ids=true, to_apply=%region_11.12 | all-reduce | flops 64 | bytes 512 | tf_op jit(solution)/shard_map/psum | solution.py:124
  547.6 92.5 %all-reduce.2.cloned.1.call-done = f32[64,128,128]{2,0,1:T(8,128)} async-done(((f32[64,128,128]{2,0,1:T(8,128)}), f32[64,128,128]{2,0,1:T(8,128)}) %all-reduce.2.cloned.1.call-update) | async-done | bytes 4194320 | tf_op jit(solution)/shard_map/psum | solution.py:124
  640.1 5.3 convert_bitcast_fusion
  645.4 11.9 %fusion.54 = bf16[32,8,128,128]{3,1,2,0:T(8,128)(2,1)} fusion(pred[256,64]{1,0:T(32,128)(4,1)S(1)} %bitcast.122, bf16[32,8,128,128]{3,2,1,0:T(8,128)(2,1)} %bitcast.112, bf16[128,8,8,128]{3,2,1,0:T(8,128)(2,1)S(1)} %get-tuple-element.195), kind=kOutput, calls=%fused_computation.85 | convolution fusion | flops 549453824 | bytes 18890752 | tf_op jit(solution)/shard_map/sc,ck->sk/dot_general | solution.py:131
  657.3 9.2 %copy.39 = bf16[32,8,128,128]{3,2,1,0:T(8,128)(2,1)} copy(bf16[32,8,128,128]{3,1,2,0:T(8,128)(2,1)} %fusion.54) | data formatting | bytes 16777216
  666.5 5.0 all-to-all-start.3
  674.5 180.9 %all-to-all-done.3 = bf16[8,32,128,128]{3,2,1,0:T(8,128)(2,1)} async-done(((bf16[8,32,128,128]{3,2,1,0:T(8,128)(2,1)}), bf16[8,32,128,128]{3,2,1,0:T(8,128)(2,1)}, u32[]{:S(2)}, u32[]{:S(2)}) %all-to-all-start.3) | async-done | bytes 8388640 | tf_op jit(solution)/shard_map/all_to_all | solution.py:138
  855.4 5.5 gather_fusion.3
  (273 shorter events, 210.1 us)
Async XLA Ops:
  7.2 69.3 %copy-start = (f32[64,9]{0,1:T(8,128)S(1)}, f32[64,9]{0,1:T(8,128)}, u32[]{:S(2)}) copy-start(f32[64,9]{0,1:T(8,128)} %param.15) | copy-start | bytes 6916
  14.5 26.1 %all-to-all-start.1 = ((bf16[8,2,1024]{2,1,0:T(2,128)(2,1)}), bf16[8,2,1024]{2,1,0:T(2,128)(2,1)S(1)}, u32[]{:S(2)}, u32[]{:S(2)}) async-start(bf16[8,2,1024]{2,1,0:T(2,128)(2,1)} %reshape.479), calls=%async_computation.1 | async-start | bytes 65536 | tf_op jit(solution)/shard_map/all_to_all | solution.py:106
  40.6 12.4 %all-to-all-start = ((bf16[8,2,1024]{2,1,0:T(2,128)(2,1)}), bf16[8,2,1024]{2,1,0:T(2,128)(2,1)S(1)}, u32[]{:S(2)}, u32[]{:S(2)}) async-start(bf16[8,2,1024]{2,1,0:T(2,128)(2,1)} %reshape.477), calls=%async_computation | async-start | bytes 65536 | tf_op jit(solution)/shard_map/all_to_all | solution.py:103
  52.9 189.1 %all-to-all-start.2 = ((bf16[8,32,128,128]{3,2,1,0:T(8,128)(2,1)}), bf16[8,32,128,128]{3,2,1,0:T(8,128)(2,1)}, u32[]{:S(2)}, u32[]{:S(2)}) async-start(bf16[8,32,128,128]{3,2,1,0:T(8,128)(2,1)} %broadcast_select_fusion), calls=%async_computation.2 | async-start | bytes 16777216 | tf_op jit(solution)/shard_map/all_to_all | solution.py:102
  58.0 582.1 %all-reduce.2.cloned.1.call-start = ((), (), s32[]{:S(2)}) async-start(), calls=%async_computation.4 | async-start | bytes 8388608 | tf_op jit(solution)/shard_map/psum | solution.py:124
  245.5 1.7 copy-start.2
  261.3 1.7 copy-start.2
  277.1 1.7 copy-start.2
  292.8 1.7 copy-start.2
  308.6 1.7 copy-start.2
  324.3 1.7 copy-start.2
  340.1 1.7 copy-start.2
  355.8 1.7 copy-start.2
  371.6 1.7 copy-start.2
  387.3 1.7 copy-start.2
  403.1 1.7 copy-start.2
  418.9 1.7 copy-start.2
  434.6 1.7 copy-start.2
  450.4 1.7 copy-start.2
  466.2 1.7 copy-start.2
  481.9 1.7 copy-start.2
  666.5 188.9 %all-to-all-start.3 = ((bf16[8,32,128,128]{3,2,1,0:T(8,128)(2,1)}), bf16[8,32,128,128]{3,2,1,0:T(8,128)(2,1)}, u32[]{:S(2)}, u32[]{:S(2)}) async-start(bf16[8,32,128,128]{3,2,1,0:T(8,128)(2,1)} %bitcast.113), calls=%async_computation.3 | async-start | bytes 16777216 | tf_op jit(solution)/shard_map/all_to_all | solution.py:138
  671.5 189.4 %copy-start.1 = (f32[64,9]{0,1:T(8,128)S(1)}, f32[64,9]{0,1:T(8,128)}, u32[]{:S(2)}) copy-start(f32[64,9]{0,1:T(8,128)} %param.15) | copy-start | bytes 6916
Sparse Core Ops, SparseCore 0:
  537.3 102.7 all-reduce.1
where the time goes:
time: 876 us; the launch traced here: 868 us
  waiting for transfers between devices  438 us (50%)
  local copies, waits for them, and re-layouts  166 us (19%)
  matrix products  115 us (13%)
  other arithmetic  89.4 us (10%)
  starting transfers between devices  33.2 us (4%)
  between operations  14.6 us (2%)
  blocking collectives  10.3 us (1%)
    all_to_all x1, waiting for transfers between devices, shards(): lax.all_to_all(difference_slots.reshape(patches, capacity, side_len, side...  181 us
    all_to_all x1, waiting for transfers between devices, shards(): lax.all_to_all(pack_slots(masked), 'patch', split_axis=0, concat_axis=0,...  165 us
    psum x1, waiting for transfers between devices, shards(): numerator, weight_sum = lax.psum((numerator, weight_sum), 'visit')  92.5 us
    dot_general x16, matrix products, match_group(): jnp.einsum('nisp,npsj->nij', left_bands, columns, preferred_element_type=...  78.8 us
    reshape x16, local copies, waits for them, and re-layouts, match_group(): columns.astype(jnp.bfloat16).reshape(number, side_len, 6, side_len)  74.8 us
    unnamed x12, local copies, waits for them, and re-layouts  35.7 us
    mul x16, other arithmetic, match_group(): coefficients[:, 3 * sigma_pos, None, None] * even_band  32.3 us
    dynamic_slice x16, local copies, waits for them, and re-layouts, match_blocks(): lax.map(one_batch, (blocks.reshape(rounds, batch_blocks, side_len, side_l...  23.8 us
  transfers between devices with their start and end apart: 5, of which 3 were waited for; matrix products, arithmetic and copies ran while one was open for 4% of the time, Pallas kernels for 0%

commit v1 on v0

--- a/solution.py
+++ b/solution.py
@@ -1,6 +1,8 @@
 import jax
 import jax.numpy as jnp
 from jax import lax
+from jax.experimental import pallas as pl
+from jax.experimental.pallas import tpu as pltpu
 from jax.sharding import PartitionSpec as P
 
 CELLS = 64
@@ -146,6 +148,305 @@
     return (coadd_part, difference)
 
 
+GROUP = 16
+HALF = 4
+ROWS = 8
+STEPS = 4
+PAIR = ROWS // STEPS
+MESH = pl.DeviceIdType.MESH
+
+
+def match_kernel(coef_ref, pixels_ref, mask_ref, right_ref, tables_ref, out_ref, wide):
+    step = pl.program_id(0)
+    per_step, side_len = pixels_ref.shape[0], pixels_ref.shape[1]
+    unit = 4
+
+    def some(part, carry):
+        first = part * unit
+        usable = (mask_ref[pl.ds(first, unit)] & 7) == 0
+        masked = jnp.where(usable, pixels_ref[pl.ds(first, unit)].astype(jnp.float32), 0.0)
+        masked = masked.astype(jnp.bfloat16).reshape(unit * side_len, side_len)
+        columns = jnp.dot(masked, right_ref[...], preferred_element_type=jnp.float32)
+        columns = columns.astype(jnp.bfloat16)
+        for n in range(unit):
+            block = step * per_step + first + n
+            left_parts = []
+            for m in range(3):
+                even, odd = tables_ref[2 * m], tables_ref[2 * m + 1]
+                left_parts.append(
+                    (coef_ref[block, 3 * m] * even + coef_ref[block, 3 * m + 1] * odd).astype(jnp.bfloat16)
+                )
+                left_parts.append((coef_ref[block, 3 * m + 2] * even).astype(jnp.bfloat16))
+            left = jnp.concatenate(left_parts, axis=1)
+            own = columns[n * side_len : (n + 1) * side_len]
+            stacked = jnp.concatenate(
+                [own[:, p * side_len : (p + 1) * side_len] for p in range(6)], axis=0
+            )
+            start = pl.multiple_of((first + n) * side_len, side_len)
+            wide[pl.ds(start, side_len), :] = jnp.dot(left, stacked, preferred_element_type=jnp.float32)
+        return carry
+
+    lax.fori_loop(0, per_step // unit, some, 0)
+    for g in range(GROUP):
+        for r in range(ROWS):
+            rows = wide[pl.ds(g * ROWS + r, per_step, stride=side_len), :]
+            lane = r % PAIR * side_len
+            out_ref[r // PAIR, g, :, lane : lane + side_len] = rows.astype(jnp.bfloat16)
+
+
+def match_rows(pixels, mask_bits, coefficients, right_bands, tables):
+    blocks, side_len = pixels.shape[0], pixels.shape[1]
+    per_step = 16
+    return pl.pallas_call(
+        match_kernel,
+        grid=(blocks // per_step,),
+        in_specs=[
+            pl.BlockSpec(memory_space=pltpu.SMEM),
+            pl.BlockSpec((per_step, side_len, side_len), lambda i: (i, 0, 0)),
+            pl.BlockSpec((per_step, side_len, side_len), lambda i: (i, 0, 0)),
+            pl.BlockSpec(right_bands.shape, lambda i: (0, 0)),
+            pl.BlockSpec(tables.shape, lambda i: (0, 0, 0)),
+        ],
+        out_specs=pl.BlockSpec((STEPS, GROUP, per_step, PAIR * side_len), lambda i: (0, 0, i, 0)),
+        out_shape=jax.ShapeDtypeStruct((STEPS, GROUP, blocks, PAIR * side_len), jnp.bfloat16),
+        scratch_shapes=[pltpu.VMEM((per_step * side_len, side_len), jnp.float32)],
+        compiler_params=pltpu.CompilerParams(vmem_limit_bytes=40 * 2**20),
+    )(coefficients, pixels, mask_bits, right_bands, tables)
+
+
+def trade_kernel(
+    rows_ref, seg_row_ref, weight_row_ref, seg_column_ref, scale_ref,
+    coadd_ref, difference_ref,
+    held, sums, sums_out, sums_in, templates, coadd_in, diffs, diffs_in, weights, picks, wide,
+    send_rows, recv_rows, send_sums, recv_sums, send_coadd, recv_coadd, send_diffs, recv_diffs,
+):
+    side_len = wide.shape[1]
+    blocks = held.shape[2]
+    total = GROUP * blocks
+    cells = weights.shape[0]
+    visit, patch = lax.axis_index("visit"), lax.axis_index("patch")
+    half, place = patch // HALF, patch % HALF
+    me = visit * HALF + place
+
+    def device_of(index):
+        return (index // HALF, half * HALF + index % HALF)
+
+    partner = (visit, (1 - half) * HALF + place)
+    barrier = pltpu.get_barrier_semaphore()
+
+    def peers(act):
+        def one(turn, carry):
+            act((me + turn) % GROUP)
+            return carry
+
+        lax.fori_loop(1, GROUP, one, 0)
+
+    peers(
+        lambda peer: pl.semaphore_signal(
+            barrier, inc=1, device_id=device_of(peer), device_id_type=MESH
+        )
+    )
+    pl.semaphore_signal(barrier, inc=1, device_id=partner, device_id_type=MESH)
+    pl.semaphore_wait(barrier, GROUP)
+
+    def rows_copy(step, peer, slot):
+        return pltpu.make_async_remote_copy(
+            src_ref=rows_ref.at[step, peer], dst_ref=held.at[step, slot],
+            send_sem=send_rows.at[step, peer], recv_sem=recv_rows.at[step, slot],
+            device_id=device_of(peer), device_id_type=MESH,
+        )
+
+    def sums_copy(step):
+        return pltpu.make_async_remote_copy(
+            src_ref=sums_out.at[step], dst_ref=sums_in.at[step],
+            send_sem=send_sums.at[step], recv_sem=recv_sums.at[step],
+            device_id=partner, device_id_type=MESH,
+        )
+
+    def coadd_copy(step, peer, slot):
+        start = pl.multiple_of((half * HALF + peer) * CELLS, CELLS)
+        return pltpu.make_async_remote_copy(
+            src_ref=templates.at[step, pl.ds(start, CELLS)], dst_ref=coadd_in.at[step, slot],
+            send_sem=send_coadd.at[step, peer], recv_sem=recv_coadd.at[step, slot],
+            device_id=(visit, half * HALF + peer), device_id_type=MESH,
+        )
+
+    def diffs_copy(step, peer, slot):
+        return pltpu.make_async_remote_copy(
+            src_ref=diffs.at[step, peer], dst_ref=diffs_in.at[step, slot],
+            send_sem=send_diffs.at[step, peer], recv_sem=recv_diffs.at[step, slot],
+            device_id=device_of(peer), device_id_type=MESH,
+        )
+
+    for step in range(STEPS):
+        peers(lambda peer: rows_copy(step, peer, me).start())
+        held[step, pl.ds(me, 1)] = rows_ref[step, pl.ds(me, 1)]
+
+    strip = 64
+
+    def make_weights(part, carry):
+        start = pl.multiple_of(part * strip, strip)
+        cell = lax.broadcasted_iota(jnp.int32, (strip, total), 0) + start
+        chosen = jnp.where(cell == seg_row_ref[...], weight_row_ref[...], 0.0)
+        weights[pl.ds(start, strip), :] = chosen.astype(jnp.bfloat16)
+        return carry
+
+    lax.fori_loop(0, cells // strip, make_weights, 0)
+
+    def make_picks(part, carry):
+        start = pl.multiple_of(part * strip, strip)
+        cell = lax.broadcasted_iota(jnp.int32, (strip, cells), 1)
+        chosen = jnp.where(cell == seg_column_ref[pl.ds(start, strip), :], 1.0, 0.0)
+        picks[pl.ds(start, strip), :] = chosen.astype(jnp.bfloat16)
+        return carry
+
+    lax.fori_loop(0, total // strip, make_picks, 0)
+
+    for step in range(STEPS):
+        peers(lambda peer: rows_copy(step, peer, peer).wait_recv())
+        flat = held[step].reshape(total, PAIR * side_len)
+        part_sum = jnp.dot(weights[...], flat, preferred_element_type=jnp.float32)
+        sums[step] = part_sum
+        sums_out[step] = part_sum.astype(jnp.bfloat16)
+        sums_copy(step).start()
+
+    for step in range(STEPS):
+        sums_copy(step).wait_recv()
+        template = (sums[step] + sums_in[step].astype(jnp.float32)) * scale_ref[...]
+        templates[step] = template.astype(jnp.bfloat16)
+        flat = held[step].reshape(total, PAIR * side_len)
+        chosen = jnp.dot(picks[...], templates[step], preferred_element_type=jnp.float32)
+        change = (flat.astype(jnp.float32) - chosen).astype(jnp.bfloat16)
+        diffs[step] = change.reshape(GROUP, blocks, PAIR * side_len)
+        peers(lambda peer: diffs_copy(step, peer, me).start())
+        for turn in range(1, HALF):
+            coadd_copy(step, (place + turn) % HALF, place).start()
+        start = pl.multiple_of(patch * CELLS, CELLS)
+        coadd_in[step, pl.ds(place, 1)] = templates[step, pl.ds(start, CELLS)].reshape(
+            1, CELLS, PAIR * side_len
+        )
+        diffs_in[step, pl.ds(me, 1)] = diffs[step, pl.ds(me, 1)]
+
+    rows_here = HALF * ROWS
+    for step in range(STEPS):
+        peers(lambda peer: diffs_copy(step, peer, peer).wait_recv())
+
+        def spread(source, carry):
+            values = diffs_in[step, source].astype(jnp.float32)
+            for k in range(PAIR):
+                row = source * ROWS + step * PAIR + k
+                wide[pl.ds(row, blocks, stride=side_len), :] = values[
+                    :, k * side_len : (k + 1) * side_len
+                ]
+            return carry
+
+        lax.fori_loop(0, GROUP, spread, 0)
+        for turn in range(1, HALF):
+            peer = (place + turn) % HALF
+            coadd_copy(step, peer, peer).wait_recv()
+        for source in range(HALF):
+            values = coadd_in[step, source].astype(jnp.float32)
+            for k in range(PAIR):
+                row = source * ROWS + step * PAIR + k
+                coadd_ref[pl.ds(row, CELLS, stride=rows_here), :] = values[
+                    :, k * side_len : (k + 1) * side_len
+                ]
+
+    def narrow(part, carry):
+        start = pl.multiple_of(part * 512, 512)
+        difference_ref[pl.ds(start, 512), :] = wide[pl.ds(start, 512), :].astype(jnp.bfloat16)
+        return carry
+
+    lax.fori_loop(0, wide.shape[0] // 512, narrow, 0)
+
+    for step in range(STEPS):
+        peers(lambda peer: rows_copy(step, peer, me).wait_send())
+        sums_copy(step).wait_send()
+        peers(lambda peer: diffs_copy(step, peer, me).wait_send())
+        for turn in range(1, HALF):
+            coadd_copy(step, (place + turn) % HALF, place).wait_send()
+
+
+def trade(rows, seg_row, weight_row, seg_column, scale, side_len):
+    blocks, width = rows.shape[2], rows.shape[3]
+    total = GROUP * blocks
+    cells = scale.shape[0]
+    bf16, f32 = jnp.bfloat16, jnp.float32
+    dma = pltpu.SemaphoreType.DMA
+    return pl.pallas_call(
+        trade_kernel,
+        in_specs=[pl.BlockSpec(memory_space=pltpu.VMEM)] * 5,
+        out_specs=[pl.BlockSpec(memory_space=pltpu.VMEM)] * 2,
+        out_shape=[
+            jax.ShapeDtypeStruct((CELLS * HALF * ROWS, side_len), f32),
+            jax.ShapeDtypeStruct((blocks * side_len, side_len), bf16),
+        ],
+        scratch_shapes=[
+            pltpu.VMEM((STEPS, GROUP, blocks, width), bf16),
+            pltpu.VMEM((STEPS, cells, width), f32),
+            pltpu.VMEM((STEPS, cells, width), bf16),
+            pltpu.VMEM((STEPS, cells, width), bf16),
+            pltpu.VMEM((STEPS, cells, width), bf16),
+            pltpu.VMEM((STEPS, HALF, CELLS, width), bf16),
+            pltpu.VMEM((STEPS, GROUP, blocks, width), bf16),
+            pltpu.VMEM((STEPS, GROUP, blocks, width), bf16),
+            pltpu.VMEM((cells, total), bf16),
+            pltpu.VMEM((total, cells), bf16),
+            pltpu.VMEM((blocks * side_len, side_len), f32),
+            dma((STEPS, GROUP)),
+            dma((STEPS, GROUP)),
+            dma((STEPS,)),
+            dma((STEPS,)),
+            dma((STEPS, HALF)),
+            dma((STEPS, HALF)),
+            dma((STEPS, GROUP)),
+            dma((STEPS, GROUP)),
+        ],
+        compiler_params=pltpu.CompilerParams(
+            collective_id=0, has_side_effects=True, vmem_limit_bytes=48 * 2**20
+        ),
+    )(rows, seg_row, weight_row, seg_column, scale)
+
+
+def row_shards(pixels, mask_bits, inv_var, owner, cell, coef_index, coef_table):
+    blocks, side_len = pixels.shape[0], pixels.shape[1]
+    patches = lax.axis_size("patch")
+    visits = lax.axis_size("visit")
+    cells = patches * CELLS
+    tables = band_tables(side_len)
+    right_bands = (
+        jnp.transpose(tables, (2, 0, 1)).reshape(side_len, 6 * side_len).astype(jnp.bfloat16)
+    )
+    weight = inv_var.astype(jnp.bfloat16).astype(jnp.float32)
+    segment = (owner * CELLS + cell).astype(jnp.float32)
+    facts = lax.all_gather(jnp.stack([segment, weight]), ("visit", "patch"), tiled=False)
+    coefficients = coef_table[coef_index]
+    rows = match_rows(pixels, mask_bits, coefficients, right_bands, tables)
+    every_segment = facts[:, 0].astype(jnp.int32).reshape(1, -1)
+    every_weight = facts[:, 1].reshape(1, -1)
+    weight_sum = jnp.sum(
+        jnp.where(jnp.arange(cells, dtype=jnp.int32)[:, None] == every_segment, every_weight, 0.0), axis=1
+    )
+    scale = (1.0 / jnp.maximum(weight_sum, 1.0))[:, None]
+    half = lax.axis_index("patch") // HALF
+    near = lax.dynamic_index_in_dim(
+        facts.reshape(visits, patches // HALF, HALF, 2, blocks), half, 1, keepdims=False
+    ).reshape(GROUP, 2, blocks)
+    near_segment = near[:, 0].astype(jnp.int32)
+    coadd, difference = trade(
+        rows,
+        near_segment.reshape(1, -1),
+        near[:, 1].reshape(1, -1),
+        near_segment.reshape(-1, 1),
+        scale,
+        side_len,
+    )
+    return (
+        coadd.reshape(CELLS, HALF * ROWS, side_len),
+        difference.reshape(blocks, side_len, side_len),
+    )
+
+
 def solution(mesh):
     placed = (
         P(("visit", "patch"), None, None),
@@ -156,8 +457,9 @@
         P(("visit", "patch")),
         P(),
     )
+    fits = mesh.shape["visit"] == GROUP // HALF and mesh.shape["patch"] == 2 * HALF
     return jax.shard_map(
-        shards,
+        row_shards if fits else shards,
         mesh=mesh,
         in_specs=placed,
         out_specs=(P("patch", "visit", None), P(("visit", "patch"), None, None)),

time: 876 us -> 156 us (0.18)
  waiting for transfers between devices: 438 us -> 0 us
  local copies, waits for them, and re-layouts: 166 us -> 6.97 us
  matrix products: 115 us -> 0 us
  Pallas kernels: 0 us -> 94.8 us
  other arithmetic: 89.4 us -> 9.08 us
  starting transfers between devices: 33.2 us -> 0 us
  blocking collectives: 10.3 us -> 43.3 us
  between operations: 14.6 us -> 0.77 us
    all_to_all x4 -> x0, waiting for transfers between devices: 346 us -> none  [the longest x1 181 us: shards(): lax.all_to_all(difference_slots.reshape(patches, capacity, side_len, side...]
    dot_general x35 -> x0, matrix products: 115 us -> none  [the longest x16 78.8 us: match_group(): jnp.einsum('nisp,npsj->nij', left_bands, columns, preferred_element_type=...]
    pallas_call x0 -> x2, Pallas kernels: none -> 94.8 us  [the longest x1 80.8 us: trade(): pl.pallas_call(trade_kernel, in_specs=[pl.BlockSpec(memory_space=pltpu.VM...]
    psum x1 -> x0, waiting for transfers between devices: 92.5 us -> none  [shards(): numerator, weight_sum = lax.psum((numerator, weight_sum), 'visit')]
    reshape x16 -> x0, local copies, waits for them, and re-layouts: 74.8 us -> none  [match_group(): columns.astype(jnp.bfloat16).reshape(number, side_len, 6, side_len)]
    all_gather x0 -> x1, blocking collectives: none -> 43.3 us  [row_shards(): lax.all_gather(jnp.stack([segment, weight]), ('visit', 'patch'), tiled=Fa...]
    mul x16 -> x0, other arithmetic: 32.3 us -> none  [match_group(): coefficients[:, 3 * sigma_pos, None, None] * even_band]
    unnamed x12 -> x7, local copies, waits for them, and re-layouts: 35.7 us -> 5.27 us
  transfers between devices with their start and end apart: 5 -> 0, of which waited for: 3 -> 0; matrix products, arithmetic and copies ran while one was open for 4% -> 0% of each run, Pallas kernels for 0% -> 0%
where the time goes in v1:
time: 156 us; the launch traced here: 155 us
  Pallas kernels  94.8 us (61%)
  blocking collectives  43.3 us (28%)
  other arithmetic  9.08 us (6%)
  local copies, waits for them, and re-layouts  6.97 us (4%)
    pallas_call x1, Pallas kernels, trade(): pl.pallas_call(trade_kernel, in_specs=[pl.BlockSpec(memory_space=pltpu.VM...  80.8 us
    all_gather x1, blocking collectives, row_shards(): lax.all_gather(jnp.stack([segment, weight]), ('visit', 'patch'), tiled=Fa...  43.3 us
    pallas_call x1, Pallas kernels, match_rows(): pl.pallas_call(match_kernel, grid=(blocks // per_step,), in_specs=[pl.Blo...  14 us
    unnamed x7, local copies, waits for them, and re-layouts  5.27 us
    unnamed x6, other arithmetic  3.77 us

profile of v1, /device:TPU:0, one launch (start us, length us, event | category | flops | bytes accessed | tf_op | source)
XLA Modules:
  0.0 154.9 jit_solution(14899874763700063228)
XLA Ops:
  0.6 0.0 copy-start.1
  0.6 0.6 exponential_reduce_fusion.2
  1.3 0.6 exponential_reduce_fusion.1
  1.9 0.7 exponential_reduce_fusion
  2.6 0.7 bitcast_convert_fusion
  3.2 0.7 convert_bitcast_fusion
  3.9 0.7 compare_select_fusion
  4.6 43.3 %all-gather.1 = f32[32,2,64]{2,1,0:T(2,128)S(1)} all-gather(f32[1,2,64]{2,1,0:T(2,128)S(1)} %maximum_bitcast_fusion), channel_id=2, replica_groups=mesh['visit'=4,'patch'=8] {'visit','patch'}, dimensions={0}, use_global_device_ids=true | all-gather | bytes 16896 | tf_op jit(solution)/shard_map/all_gather | solution.py:422
  47.9 0.1 reshape_squeeze.4.weight_row_ref
  48.0 0.1 convert_element_type.89.seg_row_ref
  48.0 0.1 slice_reduce_fusion
  48.1 0.1 fusion.21
  48.2 0.1 convert_element_type.92
  48.2 0.1 broadcast_in_dim.29
  48.3 0.5 select_reduce_fusion
  48.8 0.8 copy.22
  49.6 0.6 gather_fusion
  50.2 0.1 copy.26.scale_ref
  50.3 0.7 fusion.20
  51.1 0.7 fusion.13
  51.8 0.7 fusion.19
  52.6 0.7 fusion.15
  53.4 0.8 fusion.18
  54.1 0.8 fusion.17.tables_ref
  55.0 0.1 copy.23.right_ref
  55.1 0.5 convert_element_type.93.seg_column_ref
  55.6 0.0 copy-start
  55.6 2.2 %copy-done = s32[64,128,128]{2,1,0:T(8,128)S(1)} copy-done((s32[64,128,128]{2,1,0:T(8,128)S(1)}, s32[64,128,128]{2,1,0:T(8,128)}, u32[]{:S(2)}) %copy-start) | copy-done | bytes 4194328
  57.8 14.0 %shard_map.86.rows_ref = bf16[4,16,64,256]{3,2,1,0:T(8,128)(2,1)S(1)} custom-call(f32[64,9]{1,0:T(8,128)S(1)} %gather_fusion, bf16[64,128,128]{2,1,0:T(8,128)(2,1)S(1)} %copy-done.1, s32[64,128,128]{2,1,0:T(8,128)S(1)} %copy-done, bf16[128,768]{1,0:T(8,128)(2,1)S(1)} %copy.23.right_ref, f32[6,128,128]{2,1,0:T(8,128)S(1)} %fusion.17.tables_ref), custom_call_target="tpu_custom_call" | custom-call | tf_op jit(solution)/shard_map/pallas_call | solution.py:200
  71.8 80.8 %shard_map.87 = (f32[2048,128]{1,0:T(8,128)S(1)}, bf16[8192,128]{1,0:T(8,128)(2,1)S(1)}) custom-call(bf16[4,16,64,256]{3,2,1,0:T(8,128)(2,1)S(1)} %shard_map.86.rows_ref, s32[1,1024]{1,0:T(1,128)S(1)} %convert_element_type.89.seg_row_ref, f32[1,1024]{1,0:T(1,128)S(1)} %reshape_squeeze.4.weight_row_ref, s32[1024,1]{1,0:T(8,128)S(1)} %convert_element_type.93.seg_column_ref, ...), custom_call_target="tpu_custom_call" | custom-call | tf_op jit(solution)/shard_map/pallas_call | solution.py:376
  152.6 1.0 copy.34
  153.6 1.3 copy.35
  (9 shorter events, 0.1 us)
Async XLA Ops:
  0.6 55.0 %copy-start.1 = (bf16[64,128,128]{2,1,0:T(8,128)(2,1)S(1)}, bf16[64,128,128]{2,1,0:T(8,128)(2,1)}, u32[]{:S(2)}) copy-start(bf16[64,128,128]{2,1,0:T(8,128)(2,1)} %pixels_ref.1) | copy-start | bytes 6291460
  55.6 2.2 %copy-start = (s32[64,128,128]{2,1,0:T(8,128)S(1)}, s32[64,128,128]{2,1,0:T(8,128)}, u32[]{:S(2)}) copy-start(s32[64,128,128]{2,1,0:T(8,128)} %mask_ref.1) | copy-start | bytes 12582916

commit v2 on v1

--- a/solution.py
+++ b/solution.py
@@ -1,5 +1,6 @@
 import jax
 import jax.numpy as jnp
+import numpy as np
 from jax import lax
 from jax.experimental import pallas as pl
 from jax.experimental.pallas import tpu as pltpu
@@ -156,12 +157,110 @@
 MESH = pl.DeviceIdType.MESH
 
 
-def match_kernel(coef_ref, pixels_ref, mask_ref, right_ref, tables_ref, out_ref, wide):
-    step = pl.program_id(0)
-    per_step, side_len = pixels_ref.shape[0], pixels_ref.shape[1]
+def fixed_bands(side_len):
+    reach = KSIZE // 2
+    position = np.arange(side_len, dtype=np.float32)
+    offset = position[:, None] - position[None, :]
+    taps = np.arange(-reach, reach + 1).astype(np.float32)
+    tables = []
+    for spread in gauss_widths:
+        spread = np.float32(spread)
+        total = np.sum(np.exp(-taps * taps / (2 * spread * spread)))
+        even = np.where(np.abs(offset) <= reach, np.exp(-offset * offset / (2 * spread * spread)) / total, 0)
+        tables.append(even.astype(np.float32))
+        tables.append((even * offset / spread).astype(np.float32))
+    return np.stack(tables)
+
+
+def trade_kernel(
+    index_ref, table_ref, pixels_ref, mask_ref, facts_ref, right_ref, bands_ref,
+    coadd_ref, difference_ref,
+    rows, held, sums, sums_out, sums_in, templates, coadd_in, diffs, diffs_in, weights, picks, wide,
+    facts_in, weight_rows, total_out, total_in, scale,
+    send_early, recv_early, send_rows, recv_rows, send_facts, recv_facts, send_total, recv_total,
+    send_sums, recv_sums, send_coadd, recv_coadd, send_diffs, recv_diffs,
+):
+    blocks, side_len = pixels_ref.shape[0], pixels_ref.shape[1]
+    total = GROUP * blocks
+    early = blocks // 2
+    cells = weights.shape[0]
+    visit, patch = lax.axis_index("visit"), lax.axis_index("patch")
+    half, place = patch // HALF, patch % HALF
+    me = visit * HALF + place
+
+    def device_of(index):
+        return (index // HALF, half * HALF + index % HALF)
+
+    partner = (visit, (1 - half) * HALF + place)
+    barrier = pltpu.get_barrier_semaphore()
+
+    def peers(act):
+        def one(turn, carry):
+            act((me + turn) % GROUP)
+            return carry
+
+        lax.fori_loop(1, GROUP, one, 0)
+
+    peers(
+        lambda peer: pl.semaphore_signal(
+            barrier, inc=1, device_id=device_of(peer), device_id_type=MESH
+        )
+    )
+    pl.semaphore_signal(barrier, inc=1, device_id=partner, device_id_type=MESH)
+
+    def facts_copy(peer, slot):
+        return pltpu.make_async_remote_copy(
+            src_ref=facts_ref, dst_ref=facts_in.at[slot],
+            send_sem=send_facts.at[peer], recv_sem=recv_facts.at[slot],
+            device_id=device_of(peer), device_id_type=MESH,
+        )
+
+    def early_copy(peer, slot):
+        return pltpu.make_async_remote_copy(
+            src_ref=rows.at[:, peer, pl.ds(0, early)], dst_ref=held.at[:, slot, pl.ds(0, early)],
+            send_sem=send_early.at[peer], recv_sem=recv_early.at[slot],
+            device_id=device_of(peer), device_id_type=MESH,
+        )
+
+    def rows_copy(step, peer, slot):
+        return pltpu.make_async_remote_copy(
+            src_ref=rows.at[step, peer, pl.ds(early, blocks - early)],
+            dst_ref=held.at[step, slot, pl.ds(early, blocks - early)],
+            send_sem=send_rows.at[step, peer], recv_sem=recv_rows.at[step, slot],
+            device_id=device_of(peer), device_id_type=MESH,
+        )
+
+    def total_copy():
+        return pltpu.make_async_remote_copy(
+            src_ref=total_out, dst_ref=total_in, send_sem=send_total, recv_sem=recv_total,
+            device_id=partner, device_id_type=MESH,
+        )
+
+    def sums_copy(step):
+        return pltpu.make_async_remote_copy(
+            src_ref=sums_out.at[step], dst_ref=sums_in.at[step],
+            send_sem=send_sums.at[step], recv_sem=recv_sums.at[step],
+            device_id=partner, device_id_type=MESH,
+        )
+
+    def coadd_copy(step, peer, slot):
+        start = pl.multiple_of((half * HALF + peer) * CELLS, CELLS)
+        return pltpu.make_async_remote_copy(
+            src_ref=templates.at[step, pl.ds(start, CELLS)], dst_ref=coadd_in.at[step, slot],
+            send_sem=send_coadd.at[step, peer], recv_sem=recv_coadd.at[step, slot],
+            device_id=(visit, half * HALF + peer), device_id_type=MESH,
+        )
+
+    def diffs_copy(step, peer, slot):
+        return pltpu.make_async_remote_copy(
+            src_ref=diffs.at[step, peer], dst_ref=diffs_in.at[step, slot],
+            send_sem=send_diffs.at[step, peer], recv_sem=recv_diffs.at[step, slot],
+            device_id=device_of(peer), device_id_type=MESH,
+        )
+
     unit = 4
 
-    def some(part, carry):
+    def match_unit(part, carry):
         first = part * unit
         usable = (mask_ref[pl.ds(first, unit)] & 7) == 0
         masked = jnp.where(usable, pixels_ref[pl.ds(first, unit)].astype(jnp.float32), 0.0)
@@ -169,14 +268,13 @@
         columns = jnp.dot(masked, right_ref[...], preferred_element_type=jnp.float32)
         columns = columns.astype(jnp.bfloat16)
         for n in range(unit):
-            block = step * per_step + first + n
+            kernel_set = index_ref[first + n]
             left_parts = []
             for m in range(3):
-                even, odd = tables_ref[2 * m], tables_ref[2 * m + 1]
-                left_parts.append(
-                    (coef_ref[block, 3 * m] * even + coef_ref[block, 3 * m + 1] * odd).astype(jnp.bfloat16)
-                )
-                left_parts.append((coef_ref[block, 3 * m + 2] * even).astype(jnp.bfloat16))
+                even, odd = bands_ref[2 * m], bands_ref[2 * m + 1]
+                coef = [table_ref[kernel_set, 3 * m + t] for t in range(3)]
+                left_parts.append((coef[0] * even + coef[1] * odd).astype(jnp.bfloat16))
+                left_parts.append((coef[2] * even).astype(jnp.bfloat16))
             left = jnp.concatenate(left_parts, axis=1)
             own = columns[n * side_len : (n + 1) * side_len]
             stacked = jnp.concatenate(
@@ -186,121 +284,52 @@
             wide[pl.ds(start, side_len), :] = jnp.dot(left, stacked, preferred_element_type=jnp.float32)
         return carry
 
-    lax.fori_loop(0, per_step // unit, some, 0)
-    for g in range(GROUP):
-        for r in range(ROWS):
-            rows = wide[pl.ds(g * ROWS + r, per_step, stride=side_len), :]
-            lane = r % PAIR * side_len
-            out_ref[r // PAIR, g, :, lane : lane + side_len] = rows.astype(jnp.bfloat16)
-
-
-def match_rows(pixels, mask_bits, coefficients, right_bands, tables):
-    blocks, side_len = pixels.shape[0], pixels.shape[1]
-    per_step = 16
-    return pl.pallas_call(
-        match_kernel,
-        grid=(blocks // per_step,),
-        in_specs=[
-            pl.BlockSpec(memory_space=pltpu.SMEM),
-            pl.BlockSpec((per_step, side_len, side_len), lambda i: (i, 0, 0)),
-            pl.BlockSpec((per_step, side_len, side_len), lambda i: (i, 0, 0)),
-            pl.BlockSpec(right_bands.shape, lambda i: (0, 0)),
-            pl.BlockSpec(tables.shape, lambda i: (0, 0, 0)),
-        ],
-        out_specs=pl.BlockSpec((STEPS, GROUP, per_step, PAIR * side_len), lambda i: (0, 0, i, 0)),
-        out_shape=jax.ShapeDtypeStruct((STEPS, GROUP, blocks, PAIR * side_len), jnp.bfloat16),
-        scratch_shapes=[pltpu.VMEM((per_step * side_len, side_len), jnp.float32)],
-        compiler_params=pltpu.CompilerParams(vmem_limit_bytes=40 * 2**20),
-    )(coefficients, pixels, mask_bits, right_bands, tables)
-
-
-def trade_kernel(
-    rows_ref, seg_row_ref, weight_row_ref, seg_column_ref, scale_ref,
-    coadd_ref, difference_ref,
-    held, sums, sums_out, sums_in, templates, coadd_in, diffs, diffs_in, weights, picks, wide,
-    send_rows, recv_rows, send_sums, recv_sums, send_coadd, recv_coadd, send_diffs, recv_diffs,
-):
-    side_len = wide.shape[1]
-    blocks = held.shape[2]
-    total = GROUP * blocks
-    cells = weights.shape[0]
-    visit, patch = lax.axis_index("visit"), lax.axis_index("patch")
-    half, place = patch // HALF, patch % HALF
-    me = visit * HALF + place
-
-    def device_of(index):
-        return (index // HALF, half * HALF + index % HALF)
-
-    partner = (visit, (1 - half) * HALF + place)
-    barrier = pltpu.get_barrier_semaphore()
-
-    def peers(act):
-        def one(turn, carry):
-            act((me + turn) % GROUP)
+    def match_part(first, number):
+        lax.fori_loop(first // unit, (first + number) // unit, match_unit, 0)
+
+        def gather_rows(g, carry):
+            for r in range(ROWS):
+                start = first * side_len + g * ROWS + r
+                values = wide[pl.ds(start, number, stride=side_len), :].astype(jnp.bfloat16)
+                lane = r % PAIR * side_len
+                rows[r // PAIR, g, pl.ds(first, number), lane : lane + side_len] = values
             return carry
 
-        lax.fori_loop(1, GROUP, one, 0)
-
-    peers(
-        lambda peer: pl.semaphore_signal(
-            barrier, inc=1, device_id=device_of(peer), device_id_type=MESH
-        )
-    )
-    pl.semaphore_signal(barrier, inc=1, device_id=partner, device_id_type=MESH)
+        lax.fori_loop(0, GROUP, gather_rows, 0)
+
+    match_part(0, early)
     pl.semaphore_wait(barrier, GROUP)
-
-    def rows_copy(step, peer, slot):
-        return pltpu.make_async_remote_copy(
-            src_ref=rows_ref.at[step, peer], dst_ref=held.at[step, slot],
-            send_sem=send_rows.at[step, peer], recv_sem=recv_rows.at[step, slot],
-            device_id=device_of(peer), device_id_type=MESH,
-        )
-
-    def sums_copy(step):
-        return pltpu.make_async_remote_copy(
-            src_ref=sums_out.at[step], dst_ref=sums_in.at[step],
-            send_sem=send_sums.at[step], recv_sem=recv_sums.at[step],
-            device_id=partner, device_id_type=MESH,
-        )
-
-    def coadd_copy(step, peer, slot):
-        start = pl.multiple_of((half * HALF + peer) * CELLS, CELLS)
-        return pltpu.make_async_remote_copy(
-            src_ref=templates.at[step, pl.ds(start, CELLS)], dst_ref=coadd_in.at[step, slot],
-            send_sem=send_coadd.at[step, peer], recv_sem=recv_coadd.at[step, slot],
-            device_id=(visit, half * HALF + peer), device_id_type=MESH,
-        )
-
-    def diffs_copy(step, peer, slot):
-        return pltpu.make_async_remote_copy(
-            src_ref=diffs.at[step, peer], dst_ref=diffs_in.at[step, slot],
-            send_sem=send_diffs.at[step, peer], recv_sem=recv_diffs.at[step, slot],
-            device_id=device_of(peer), device_id_type=MESH,
-        )
-
+    peers(lambda peer: facts_copy(peer, me).start())
+    peers(lambda peer: early_copy(peer, me).start())
+    match_part(early, blocks - early)
     for step in range(STEPS):
         peers(lambda peer: rows_copy(step, peer, me).start())
-        held[step, pl.ds(me, 1)] = rows_ref[step, pl.ds(me, 1)]
-
-    strip = 64
-
-    def make_weights(part, carry):
-        start = pl.multiple_of(part * strip, strip)
-        cell = lax.broadcasted_iota(jnp.int32, (strip, total), 0) + start
-        chosen = jnp.where(cell == seg_row_ref[...], weight_row_ref[...], 0.0)
-        weights[pl.ds(start, strip), :] = chosen.astype(jnp.bfloat16)
+        held[step, pl.ds(me, 1)] = rows[step, pl.ds(me, 1)]
+
+    facts_in[pl.ds(me, 1)] = facts_ref[...].reshape((1,) + facts_ref.shape)
+    peers(lambda peer: facts_copy(peer, peer).wait_recv())
+    lanes = 2 * blocks
+
+    def make_pickers(pair, carry):
+        first_lanes = lax.broadcasted_iota(jnp.int32, (1, lanes), 1) < blocks
+        segment = jnp.where(first_lanes, facts_in[2 * pair, 0:1, :], facts_in[2 * pair + 1, 0:1, :])
+        weight = jnp.where(first_lanes, facts_in[2 * pair, 1:2, :], facts_in[2 * pair + 1, 1:2, :])
+        start = pl.multiple_of(pair * lanes, lanes)
+        cell = lax.broadcasted_iota(jnp.int32, (cells, lanes), 0).astype(jnp.float32)
+        weights[:, pl.ds(start, lanes)] = jnp.where(cell == segment, weight, 0.0).astype(jnp.bfloat16)
+        weight_rows[:, pl.ds(start, lanes)] = jnp.broadcast_to(weight, (16, lanes)).astype(jnp.bfloat16)
+        segment_column = jnp.broadcast_to(segment, (lanes, lanes)).T
+        for c in range(cells // lanes):
+            cell = lax.broadcasted_iota(jnp.int32, (lanes, lanes), 1) + c * lanes
+            chosen = jnp.where(cell.astype(jnp.float32) == segment_column, 1.0, 0.0)
+            picks[pl.ds(start, lanes), c * lanes : (c + 1) * lanes] = chosen.astype(jnp.bfloat16)
         return carry
 
-    lax.fori_loop(0, cells // strip, make_weights, 0)
-
-    def make_picks(part, carry):
-        start = pl.multiple_of(part * strip, strip)
-        cell = lax.broadcasted_iota(jnp.int32, (strip, cells), 1)
-        chosen = jnp.where(cell == seg_column_ref[pl.ds(start, strip), :], 1.0, 0.0)
-        picks[pl.ds(start, strip), :] = chosen.astype(jnp.bfloat16)
-        return carry
-
-    lax.fori_loop(0, total // strip, make_picks, 0)
+    lax.fori_loop(0, GROUP // 2, make_pickers, 0)
+    part_total = jnp.dot(weight_rows[...], picks[...], preferred_element_type=jnp.float32)
+    total_out[...] = part_total[0:8]
+    total_copy().start()
+    peers(lambda peer: early_copy(peer, peer).wait_recv())
 
     for step in range(STEPS):
         peers(lambda peer: rows_copy(step, peer, peer).wait_recv())
@@ -310,10 +339,19 @@
         sums_out[step] = part_sum.astype(jnp.bfloat16)
         sums_copy(step).start()
 
+    total_copy().wait_recv()
+    scale_row = 1.0 / jnp.maximum(total_out[0:1] + total_in[0:1], 1.0)
+    for c in range(cells // lanes):
+        scale[c * lanes : (c + 1) * lanes] = jnp.broadcast_to(
+            scale_row[:, c * lanes : (c + 1) * lanes], (lanes, lanes)
+        ).T
+
     for step in range(STEPS):
         sums_copy(step).wait_recv()
-        template = (sums[step] + sums_in[step].astype(jnp.float32)) * scale_ref[...]
-        templates[step] = template.astype(jnp.bfloat16)
+        whole_sum = sums[step] + sums_in[step].astype(jnp.float32)
+        for k in range(PAIR):
+            lane = slice(k * side_len, (k + 1) * side_len)
+            templates[step, :, lane] = (whole_sum[:, lane] * scale[...]).astype(jnp.bfloat16)
         flat = held[step].reshape(total, PAIR * side_len)
         chosen = jnp.dot(picks[...], templates[step], preferred_element_type=jnp.float32)
         change = (flat.astype(jnp.float32) - chosen).astype(jnp.bfloat16)
@@ -359,6 +397,9 @@
 
     lax.fori_loop(0, wide.shape[0] // 512, narrow, 0)
 
+    peers(lambda peer: facts_copy(peer, me).wait_send())
+    peers(lambda peer: early_copy(peer, me).wait_send())
+    total_copy().wait_send()
     for step in range(STEPS):
         peers(lambda peer: rows_copy(step, peer, me).wait_send())
         sums_copy(step).wait_send()
@@ -367,21 +408,29 @@
             coadd_copy(step, (place + turn) % HALF, place).wait_send()
 
 
-def trade(rows, seg_row, weight_row, seg_column, scale, side_len):
-    blocks, width = rows.shape[2], rows.shape[3]
+def row_shards(pixels, mask_bits, inv_var, owner, cell, coef_index, coef_table):
+    blocks, side_len = pixels.shape[0], pixels.shape[1]
+    cells = lax.axis_size("patch") * CELLS
     total = GROUP * blocks
-    cells = scale.shape[0]
+    width = PAIR * side_len
+    bands = fixed_bands(side_len)
+    right_bands = np.transpose(bands, (2, 0, 1)).reshape(side_len, 6 * side_len)
+    weight = inv_var.astype(jnp.bfloat16).astype(jnp.float32)
+    segment = (owner * CELLS + cell).astype(jnp.float32)
+    facts = jnp.pad(jnp.tile(jnp.stack([segment, weight]), (1, 2)), ((0, 6), (0, 0)))
     bf16, f32 = jnp.bfloat16, jnp.float32
     dma = pltpu.SemaphoreType.DMA
-    return pl.pallas_call(
+    coadd, difference = pl.pallas_call(
         trade_kernel,
-        in_specs=[pl.BlockSpec(memory_space=pltpu.VMEM)] * 5,
+        in_specs=[pl.BlockSpec(memory_space=pltpu.SMEM)] * 2
+        + [pl.BlockSpec(memory_space=pltpu.VMEM)] * 5,
         out_specs=[pl.BlockSpec(memory_space=pltpu.VMEM)] * 2,
         out_shape=[
             jax.ShapeDtypeStruct((CELLS * HALF * ROWS, side_len), f32),
             jax.ShapeDtypeStruct((blocks * side_len, side_len), bf16),
         ],
         scratch_shapes=[
+            pltpu.VMEM((STEPS, GROUP, blocks, width), bf16),
             pltpu.VMEM((STEPS, GROUP, blocks, width), bf16),
             pltpu.VMEM((STEPS, cells, width), f32),
             pltpu.VMEM((STEPS, cells, width), bf16),
@@ -393,8 +442,19 @@
             pltpu.VMEM((cells, total), bf16),
             pltpu.VMEM((total, cells), bf16),
             pltpu.VMEM((blocks * side_len, side_len), f32),
+            pltpu.VMEM((GROUP, 8, 2 * blocks), f32),
+            pltpu.VMEM((16, total), bf16),
+            pltpu.VMEM((8, cells), f32),
+            pltpu.VMEM((8, cells), f32),
+            pltpu.VMEM((cells, side_len), f32),
+            dma((GROUP,)),
+            dma((GROUP,)),
             dma((STEPS, GROUP)),
             dma((STEPS, GROUP)),
+            dma((GROUP,)),
+            dma((GROUP,)),
+            dma,
+            dma,
             dma((STEPS,)),
             dma((STEPS,)),
             dma((STEPS, HALF)),
@@ -403,43 +463,11 @@
             dma((STEPS, GROUP)),
         ],
         compiler_params=pltpu.CompilerParams(
-            collective_id=0, has_side_effects=True, vmem_limit_bytes=48 * 2**20
+            collective_id=0, has_side_effects=True, vmem_limit_bytes=56 * 2**20
         ),
-    )(rows, seg_row, weight_row, seg_column, scale)
-
-
-def row_shards(pixels, mask_bits, inv_var, owner, cell, coef_index, coef_table):
-    blocks, side_len = pixels.shape[0], pixels.shape[1]
-    patches = lax.axis_size("patch")
-    visits = lax.axis_size("visit")
-    cells = patches * CELLS
-    tables = band_tables(side_len)
-    right_bands = (
-        jnp.transpose(tables, (2, 0, 1)).reshape(side_len, 6 * side_len).astype(jnp.bfloat16)
-    )
-    weight = inv_var.astype(jnp.bfloat16).astype(jnp.float32)
-    segment = (owner * CELLS + cell).astype(jnp.float32)
-    facts = lax.all_gather(jnp.stack([segment, weight]), ("visit", "patch"), tiled=False)
-    coefficients = coef_table[coef_index]
-    rows = match_rows(pixels, mask_bits, coefficients, right_bands, tables)
-    every_segment = facts[:, 0].astype(jnp.int32).reshape(1, -1)
-    every_weight = facts[:, 1].reshape(1, -1)
-    weight_sum = jnp.sum(
-        jnp.where(jnp.arange(cells, dtype=jnp.int32)[:, None] == every_segment, every_weight, 0.0), axis=1
-    )
-    scale = (1.0 / jnp.maximum(weight_sum, 1.0))[:, None]
-    half = lax.axis_index("patch") // HALF
-    near = lax.dynamic_index_in_dim(
-        facts.reshape(visits, patches // HALF, HALF, 2, blocks), half, 1, keepdims=False
-    ).reshape(GROUP, 2, blocks)
-    near_segment = near[:, 0].astype(jnp.int32)
-    coadd, difference = trade(
-        rows,
-        near_segment.reshape(1, -1),
-        near[:, 1].reshape(1, -1),
-        near_segment.reshape(-1, 1),
-        scale,
-        side_len,
+    )(
+        coef_index, coef_table, pixels, mask_bits, facts,
+        jnp.asarray(right_bands, dtype=bf16), jnp.asarray(bands),
     )
     return (
         coadd.reshape(CELLS, HALF * ROWS, side_len),

time: 156 us -> 110 us (0.71)
  blocking collectives: 43.3 us -> 0 us
  other arithmetic: 9.08 us -> 1.34 us
  Pallas kernels: 94.8 us -> 101 us
    all_gather x1 -> x0, blocking collectives: 43.3 us -> none  [row_shards(): lax.all_gather(jnp.stack([segment, weight]), ('visit', 'patch'), tiled=Fa...]
    pallas_call x2 -> x1, Pallas kernels: 94.8 us -> 101 us  [row_shards(): pl.pallas_call(trade_kernel, in_specs=[pl.BlockSpec(memory_space=pltpu.SM...]
    unnamed x6 -> x0, other arithmetic: 3.77 us -> none
    reduce_sum x4 -> x0, other arithmetic: 2.43 us -> none  [the longest x3 1.93 us: band_tables(): jnp.sum(jnp.exp(-tap_offsets * tap_offsets / (2.0 * spread * spread)))]
    unnamed x7 -> x5, local copies, waits for them, and re-layouts: 5.27 us -> 5.13 us
where the time goes in v2:
time: 110 us; the launch traced here: 109 us
  Pallas kernels  101 us (92%)
  local copies, waits for them, and re-layouts  5.82 us (5%)
  other arithmetic  1.34 us (1%)
    pallas_call x1, Pallas kernels, row_shards(): pl.pallas_call(trade_kernel, in_specs=[pl.BlockSpec(memory_space=pltpu.SM...  101 us
    unnamed x5, local copies, waits for them, and re-layouts  5.13 us

profile of v2, /device:TPU:0, one launch (start us, length us, event | category | flops | bytes accessed | tf_op | source)
XLA Modules:
  0.0 108.9 jit_solution(6103133378324936204)
XLA Ops:
  0.6 0.7 bitcast_convert_fusion
  1.3 0.7 convert_bitcast_fusion
  2.0 0.1 tile.10
  2.1 0.6 pad.4.facts_ref
  2.7 1.4 %copy.11.table_ref = f32[64,9]{1,0:T(8,128)} copy(f32[64,9]{0,1:T(8,128)} %param.15) | data formatting | bytes 4608 | tf_op args[6]
  4.1 101.1 %shard_map.104 = (f32[2048,128]{1,0:T(8,128)}, bf16[8192,128]{1,0:T(8,128)(2,1)}) custom-call(s32[64]{0:T(128)} %index_ref.1, f32[64,9]{1,0:T(8,128)} %copy.11.table_ref, bf16[64,128,128]{2,1,0:T(8,128)(2,1)} %pixels_ref.1, s32[64,128,128]{2,1,0:T(8,128)} %mask_ref.1, f32[8,128]{1,0:T(8,128)} %pad.4.facts_ref, bf16[128,768]{1,0:T(8,128)(2,1)} %constant.9.clone.right_ref, ...), custom_call_target="tpu_custom_call" | custom-call | tf_op jit(solution)/shard_map/pallas_call | solution.py:423
  105.1 0.0 copy-start
  105.2 2.4 %copy.14 = f32[64,32,128]{2,1,0:T(8,128)} copy(f32[64,32,128]{2,1,0:T(8,128)} %bitcast.8) | data formatting | bytes 2097152
  107.6 0.0 copy-done
  107.6 1.3 %copy.15 = bf16[64,128,128]{2,1,0:T(8,128)(2,1)} copy(bf16[64,128,128]{2,1,0:T(8,128)(2,1)S(1)} %bitcast.7) | data formatting | bytes 4194304
  (2 shorter events, 0.0 us)
Async XLA Ops:
  105.1 2.4 %copy-start = (bf16[8192,128]{1,0:T(8,128)(2,1)S(1)}, bf16[8192,128]{1,0:T(8,128)(2,1)}, u32[]{:S(2)}) copy-start(bf16[8192,128]{1,0:T(8,128)(2,1)} %get-tuple-element.5) | copy-start | bytes 6291460

commit v3 on v2

--- a/solution.py
+++ b/solution.py
@@ -151,9 +151,12 @@
 
 GROUP = 16
 HALF = 4
-ROWS = 8
-STEPS = 4
+CORES = 2
+ADDERS = 8
+ROWS = 16
+STEPS = 8
 PAIR = ROWS // STEPS
+LOADS = 4
 MESH = pl.DeviceIdType.MESH
 
 
@@ -173,25 +176,33 @@
 
 
 def trade_kernel(
-    index_ref, table_ref, pixels_ref, mask_ref, facts_ref, right_ref, bands_ref,
+    index_ref, table_ref, inv_var_ref, owner_ref, cell_ref, right_ref, bands_ref, pixels_hbm, mask_hbm,
     coadd_ref, difference_ref,
-    rows, held, sums, sums_out, sums_in, templates, coadd_in, diffs, diffs_in, weights, picks, wide,
-    facts_in, weight_rows, total_out, total_in, scale,
-    send_early, recv_early, send_rows, recv_rows, send_facts, recv_facts, send_total, recv_total,
+    pixels, mask, rows, held, sums, sums_out, sums_in, templates, coadd_in, diffs, diffs_in,
+    weights, picks, wide, facts, facts_in, weight_rows, total_out, total_in, scale,
+    load_pixels, load_mask, send_rows, recv_rows, send_facts, recv_facts, send_total, recv_total,
     send_sums, recv_sums, send_coadd, recv_coadd, send_diffs, recv_diffs,
 ):
-    blocks, side_len = pixels_ref.shape[0], pixels_ref.shape[1]
+    blocks, side_len = pixels.shape[0], pixels.shape[1]
     total = GROUP * blocks
-    early = blocks // 2
     cells = weights.shape[0]
+    width = PAIR * side_len
+    lanes = 2 * blocks
+    load = blocks // LOADS
     visit, patch = lax.axis_index("visit"), lax.axis_index("patch")
-    half, place = patch // HALF, patch % HALF
+    half, place, core = patch // HALF, patch % HALF, patch % CORES
     me = visit * HALF + place
+    adder = visit * CORES + core
+    adds = patch // CORES == 1 + half
+    skip_self = jnp.where(adds, 1, 0)
 
     def device_of(index):
         return (index // HALF, half * HALF + index % HALF)
 
-    partner = (visit, (1 - half) * HALF + place)
+    def adder_of(index):
+        return (index // CORES, (1 + half) * CORES + index % CORES)
+
+    partner = (visit, (2 - half) * CORES + core)
     barrier = pltpu.get_barrier_semaphore()
 
     def peers(act):
@@ -201,33 +212,42 @@
 
         lax.fori_loop(1, GROUP, one, 0)
 
-    peers(
-        lambda peer: pl.semaphore_signal(
-            barrier, inc=1, device_id=device_of(peer), device_id_type=MESH
-        )
-    )
-    pl.semaphore_signal(barrier, inc=1, device_id=partner, device_id_type=MESH)
-
-    def facts_copy(peer, slot):
+    def adders(act):
+        def one(turn, carry):
+            act((adder + turn) % ADDERS)
+            return carry
+
+        lax.fori_loop(skip_self, ADDERS, one, 0)
+
+    def places(act):
+        def one(turn, carry):
+            act((place + turn) % HALF)
+            return carry
+
+        lax.fori_loop(1, HALF, one, 0)
+
+    def greet(device):
+        pl.semaphore_signal(barrier, inc=1, device_id=device, device_id_type=MESH)
+
+    def load_copies(part):
+        span = pl.ds(part * load, load)
+        return (
+            pltpu.make_async_copy(pixels_hbm.at[span], pixels.at[span], load_pixels.at[part]),
+            pltpu.make_async_copy(mask_hbm.at[span], mask.at[span], load_mask.at[part]),
+        )
+
+    def facts_copy(target, slot):
         return pltpu.make_async_remote_copy(
-            src_ref=facts_ref, dst_ref=facts_in.at[slot],
-            send_sem=send_facts.at[peer], recv_sem=recv_facts.at[slot],
-            device_id=device_of(peer), device_id_type=MESH,
-        )
-
-    def early_copy(peer, slot):
+            src_ref=facts, dst_ref=facts_in.at[slot],
+            send_sem=send_facts.at[target], recv_sem=recv_facts.at[slot],
+            device_id=adder_of(target), device_id_type=MESH,
+        )
+
+    def rows_copy(step, target, slot):
         return pltpu.make_async_remote_copy(
-            src_ref=rows.at[:, peer, pl.ds(0, early)], dst_ref=held.at[:, slot, pl.ds(0, early)],
-            send_sem=send_early.at[peer], recv_sem=recv_early.at[slot],
-            device_id=device_of(peer), device_id_type=MESH,
-        )
-
-    def rows_copy(step, peer, slot):
-        return pltpu.make_async_remote_copy(
-            src_ref=rows.at[step, peer, pl.ds(early, blocks - early)],
-            dst_ref=held.at[step, slot, pl.ds(early, blocks - early)],
-            send_sem=send_rows.at[step, peer], recv_sem=recv_rows.at[step, slot],
-            device_id=device_of(peer), device_id_type=MESH,
+            src_ref=rows.at[step, target], dst_ref=held.at[step, slot],
+            send_sem=send_rows.at[step, target], recv_sem=recv_rows.at[step, slot],
+            device_id=adder_of(target), device_id_type=MESH,
         )
 
     def total_copy():
@@ -258,12 +278,31 @@
             device_id=device_of(peer), device_id_type=MESH,
         )
 
+    for part in range(LOADS):
+        for copy in load_copies(part):
+            copy.start()
+
+    @pl.when(adds)
+    def _():
+        peers(lambda peer: greet(device_of(peer)))
+        greet(partner)
+
+    @pl.when(jnp.logical_not(adds))
+    def _():
+        adders(lambda target: greet(adder_of(target)))
+
+    segment = (owner_ref[...] * CELLS + cell_ref[...]).astype(jnp.float32)
+    weight = inv_var_ref[...].astype(jnp.bfloat16).astype(jnp.float32)
+    facts[...] = jnp.zeros_like(facts)
+    facts[0:1, :] = jnp.concatenate([segment, segment], axis=1)
+    facts[1:2, :] = jnp.concatenate([weight, weight], axis=1)
+
     unit = 4
 
     def match_unit(part, carry):
         first = part * unit
-        usable = (mask_ref[pl.ds(first, unit)] & 7) == 0
-        masked = jnp.where(usable, pixels_ref[pl.ds(first, unit)].astype(jnp.float32), 0.0)
+        usable = (mask[pl.ds(first, unit)] & 7) == 0
+        masked = jnp.where(usable, pixels[pl.ds(first, unit)].astype(jnp.float32), 0.0)
         masked = masked.astype(jnp.bfloat16).reshape(unit * side_len, side_len)
         columns = jnp.dot(masked, right_ref[...], preferred_element_type=jnp.float32)
         columns = columns.astype(jnp.bfloat16)
@@ -272,7 +311,7 @@
             left_parts = []
             for m in range(3):
                 even, odd = bands_ref[2 * m], bands_ref[2 * m + 1]
-                coef = [table_ref[kernel_set, 3 * m + t] for t in range(3)]
+                coef = [table_ref[3 * m + t, kernel_set] for t in range(3)]
                 left_parts.append((coef[0] * even + coef[1] * odd).astype(jnp.bfloat16))
                 left_parts.append((coef[2] * even).astype(jnp.bfloat16))
             left = jnp.concatenate(left_parts, axis=1)
@@ -284,90 +323,97 @@
             wide[pl.ds(start, side_len), :] = jnp.dot(left, stacked, preferred_element_type=jnp.float32)
         return carry
 
-    def match_part(first, number):
-        lax.fori_loop(first // unit, (first + number) // unit, match_unit, 0)
-
-        def gather_rows(g, carry):
-            for r in range(ROWS):
-                start = first * side_len + g * ROWS + r
-                values = wide[pl.ds(start, number, stride=side_len), :].astype(jnp.bfloat16)
-                lane = r % PAIR * side_len
-                rows[r // PAIR, g, pl.ds(first, number), lane : lane + side_len] = values
-            return carry
-
-        lax.fori_loop(0, GROUP, gather_rows, 0)
-
-    match_part(0, early)
-    pl.semaphore_wait(barrier, GROUP)
-    peers(lambda peer: facts_copy(peer, me).start())
-    peers(lambda peer: early_copy(peer, me).start())
-    match_part(early, blocks - early)
-    for step in range(STEPS):
-        peers(lambda peer: rows_copy(step, peer, me).start())
-        held[step, pl.ds(me, 1)] = rows[step, pl.ds(me, 1)]
-
-    facts_in[pl.ds(me, 1)] = facts_ref[...].reshape((1,) + facts_ref.shape)
-    peers(lambda peer: facts_copy(peer, peer).wait_recv())
-    lanes = 2 * blocks
-
-    def make_pickers(pair, carry):
-        first_lanes = lax.broadcasted_iota(jnp.int32, (1, lanes), 1) < blocks
-        segment = jnp.where(first_lanes, facts_in[2 * pair, 0:1, :], facts_in[2 * pair + 1, 0:1, :])
-        weight = jnp.where(first_lanes, facts_in[2 * pair, 1:2, :], facts_in[2 * pair + 1, 1:2, :])
-        start = pl.multiple_of(pair * lanes, lanes)
-        cell = lax.broadcasted_iota(jnp.int32, (cells, lanes), 0).astype(jnp.float32)
-        weights[:, pl.ds(start, lanes)] = jnp.where(cell == segment, weight, 0.0).astype(jnp.bfloat16)
-        weight_rows[:, pl.ds(start, lanes)] = jnp.broadcast_to(weight, (16, lanes)).astype(jnp.bfloat16)
-        segment_column = jnp.broadcast_to(segment, (lanes, lanes)).T
-        for c in range(cells // lanes):
-            cell = lax.broadcasted_iota(jnp.int32, (lanes, lanes), 1) + c * lanes
-            chosen = jnp.where(cell.astype(jnp.float32) == segment_column, 1.0, 0.0)
-            picks[pl.ds(start, lanes), c * lanes : (c + 1) * lanes] = chosen.astype(jnp.bfloat16)
+    for part in range(LOADS):
+        for copy in load_copies(part):
+            copy.wait()
+        lax.fori_loop(part * load // unit, (part + 1) * load // unit, match_unit, 0)
+
+    pl.semaphore_wait(barrier, jnp.where(adds, GROUP, ADDERS))
+    adders(lambda target: facts_copy(target, me).start())
+
+    def send_step(step, carry):
+        def gather_rows(target, carry):
+            for k in range(PAIR):
+                start = target * ROWS + step * PAIR + k
+                values = wide[pl.ds(start, blocks, stride=side_len), :].astype(jnp.bfloat16)
+                rows[step, target, :, k * side_len : (k + 1) * side_len] = values
+            return carry
+
+        lax.fori_loop(0, ADDERS, gather_rows, 0)
+        adders(lambda target: rows_copy(step, target, me).start())
         return carry
 
-    lax.fori_loop(0, GROUP // 2, make_pickers, 0)
-    part_total = jnp.dot(weight_rows[...], picks[...], preferred_element_type=jnp.float32)
-    total_out[...] = part_total[0:8]
-    total_copy().start()
-    peers(lambda peer: early_copy(peer, peer).wait_recv())
-
-    for step in range(STEPS):
-        peers(lambda peer: rows_copy(step, peer, peer).wait_recv())
-        flat = held[step].reshape(total, PAIR * side_len)
+    lax.fori_loop(0, STEPS, send_step, 0)
+
+    @pl.when(adds)
+    def _():
+        def keep_own(step, carry):
+            held[step, pl.ds(me, 1)] = rows[step, pl.ds(adder, 1)]
+            return carry
+
+        lax.fori_loop(0, STEPS, keep_own, 0)
+        facts_in[pl.ds(me, 1)] = facts[...].reshape((1,) + facts.shape)
+        peers(lambda peer: facts_copy(adder, peer).wait_recv())
+
+        def make_pickers(pair, carry):
+            first_lanes = lax.broadcasted_iota(jnp.int32, (1, lanes), 1) < blocks
+            segment = jnp.where(first_lanes, facts_in[2 * pair, 0:1, :], facts_in[2 * pair + 1, 0:1, :])
+            weight = jnp.where(first_lanes, facts_in[2 * pair, 1:2, :], facts_in[2 * pair + 1, 1:2, :])
+            start = pl.multiple_of(pair * lanes, lanes)
+            cell = lax.broadcasted_iota(jnp.int32, (cells, lanes), 0).astype(jnp.float32)
+            weights[:, pl.ds(start, lanes)] = jnp.where(cell == segment, weight, 0.0).astype(jnp.bfloat16)
+            weight_rows[:, pl.ds(start, lanes)] = jnp.broadcast_to(weight, (16, lanes)).astype(jnp.bfloat16)
+            segment_column = jnp.broadcast_to(segment, (lanes, lanes)).T
+            for c in range(cells // lanes):
+                cell = lax.broadcasted_iota(jnp.int32, (lanes, lanes), 1) + c * lanes
+                chosen = jnp.where(cell.astype(jnp.float32) == segment_column, 1.0, 0.0)
+                picks[pl.ds(start, lanes), c * lanes : (c + 1) * lanes] = chosen.astype(jnp.bfloat16)
+            return carry
+
+        lax.fori_loop(0, GROUP // 2, make_pickers, 0)
+        part_total = jnp.dot(weight_rows[...], picks[...], preferred_element_type=jnp.float32)
+        total_out[...] = part_total[0:8]
+        total_copy().start()
+
+    def add_up(step):
+        peers(lambda peer: rows_copy(step, adder, peer).wait_recv())
+        flat = held[step].reshape(total, width)
         part_sum = jnp.dot(weights[...], flat, preferred_element_type=jnp.float32)
         sums[step] = part_sum
         sums_out[step] = part_sum.astype(jnp.bfloat16)
         sums_copy(step).start()
 
-    total_copy().wait_recv()
-    scale_row = 1.0 / jnp.maximum(total_out[0:1] + total_in[0:1], 1.0)
-    for c in range(cells // lanes):
-        scale[c * lanes : (c + 1) * lanes] = jnp.broadcast_to(
-            scale_row[:, c * lanes : (c + 1) * lanes], (lanes, lanes)
-        ).T
-
-    for step in range(STEPS):
+    def get_scale():
+        total_copy().wait_recv()
+        scale_row = 1.0 / jnp.maximum(total_out[0:1] + total_in[0:1], 1.0)
+        for c in range(cells // lanes):
+            scale[c * lanes : (c + 1) * lanes] = jnp.broadcast_to(
+                scale_row[:, c * lanes : (c + 1) * lanes], (lanes, lanes)
+            ).T
+
+    def take_off(step):
         sums_copy(step).wait_recv()
         whole_sum = sums[step] + sums_in[step].astype(jnp.float32)
         for k in range(PAIR):
             lane = slice(k * side_len, (k + 1) * side_len)
             templates[step, :, lane] = (whole_sum[:, lane] * scale[...]).astype(jnp.bfloat16)
-        flat = held[step].reshape(total, PAIR * side_len)
+        flat = held[step].reshape(total, width)
         chosen = jnp.dot(picks[...], templates[step], preferred_element_type=jnp.float32)
         change = (flat.astype(jnp.float32) - chosen).astype(jnp.bfloat16)
-        diffs[step] = change.reshape(GROUP, blocks, PAIR * side_len)
-        peers(lambda peer: diffs_copy(step, peer, me).start())
-        for turn in range(1, HALF):
-            coadd_copy(step, (place + turn) % HALF, place).start()
+        diffs[step] = change.reshape(GROUP, blocks, width)
+        peers(lambda peer: diffs_copy(step, peer, adder).start())
+        places(lambda peer: coadd_copy(step, peer, core).start())
         start = pl.multiple_of(patch * CELLS, CELLS)
-        coadd_in[step, pl.ds(place, 1)] = templates[step, pl.ds(start, CELLS)].reshape(
-            1, CELLS, PAIR * side_len
-        )
-        diffs_in[step, pl.ds(me, 1)] = diffs[step, pl.ds(me, 1)]
-
-    rows_here = HALF * ROWS
-    for step in range(STEPS):
-        peers(lambda peer: diffs_copy(step, peer, peer).wait_recv())
+        coadd_in[step, pl.ds(core, 1)] = templates[step, pl.ds(start, CELLS)].reshape(1, CELLS, width)
+        diffs_in[step, pl.ds(adder, 1)] = diffs[step, pl.ds(me, 1)]
+
+    rows_here = CORES * ROWS
+
+    def wait_coadd(step, source):
+        coadd_copy(step, place, source).wait_recv()
+
+    def finish(step):
+        adders(lambda source: diffs_copy(step, me, source).wait_recv())
 
         def spread(source, carry):
             values = diffs_in[step, source].astype(jnp.float32)
@@ -378,11 +424,10 @@
                 ]
             return carry
 
-        lax.fori_loop(0, GROUP, spread, 0)
-        for turn in range(1, HALF):
-            peer = (place + turn) % HALF
-            coadd_copy(step, peer, peer).wait_recv()
-        for source in range(HALF):
+        lax.fori_loop(0, ADDERS, spread, 0)
+        wait_coadd(step, 1 - core)
+        pl.when(jnp.logical_not(adds))(lambda: wait_coadd(step, core))
+        for source in range(CORES):
             values = coadd_in[step, source].astype(jnp.float32)
             for k in range(PAIR):
                 row = source * ROWS + step * PAIR + k
@@ -390,6 +435,17 @@
                     :, k * side_len : (k + 1) * side_len
                 ]
 
+    lag = 2
+
+    def one_step(step, carry):
+        pl.when(adds & (step < STEPS))(lambda: add_up(step))
+        pl.when(adds & (step == 1))(get_scale)
+        pl.when(adds & (step >= 1) & (step <= STEPS))(lambda: take_off(step - 1))
+        pl.when(step >= lag)(lambda: finish(step - lag))
+        return carry
+
+    lax.fori_loop(0, STEPS + lag, one_step, 0)
+
     def narrow(part, carry):
         start = pl.multiple_of(part * 512, 512)
         difference_ref[pl.ds(start, 512), :] = wide[pl.ds(start, 512), :].astype(jnp.bfloat16)
@@ -397,15 +453,25 @@
 
     lax.fori_loop(0, wide.shape[0] // 512, narrow, 0)
 
-    peers(lambda peer: facts_copy(peer, me).wait_send())
-    peers(lambda peer: early_copy(peer, me).wait_send())
-    total_copy().wait_send()
-    for step in range(STEPS):
-        peers(lambda peer: rows_copy(step, peer, me).wait_send())
-        sums_copy(step).wait_send()
-        peers(lambda peer: diffs_copy(step, peer, me).wait_send())
-        for turn in range(1, HALF):
-            coadd_copy(step, (place + turn) % HALF, place).wait_send()
+    adders(lambda target: facts_copy(target, me).wait_send())
+
+    def sent_rows(step, carry):
+        adders(lambda target: rows_copy(step, target, me).wait_send())
+        return carry
+
+    lax.fori_loop(0, STEPS, sent_rows, 0)
+
+    @pl.when(adds)
+    def _():
+        total_copy().wait_send()
+
+        def sent(step, carry):
+            sums_copy(step).wait_send()
+            peers(lambda peer: diffs_copy(step, peer, adder).wait_send())
+            places(lambda peer: coadd_copy(step, peer, core).wait_send())
+            return carry
+
+        lax.fori_loop(0, STEPS, sent, 0)
 
 
 def row_shards(pixels, mask_bits, inv_var, owner, cell, coef_index, coef_table):
@@ -415,62 +481,63 @@
     width = PAIR * side_len
     bands = fixed_bands(side_len)
     right_bands = np.transpose(bands, (2, 0, 1)).reshape(side_len, 6 * side_len)
-    weight = inv_var.astype(jnp.bfloat16).astype(jnp.float32)
-    segment = (owner * CELLS + cell).astype(jnp.float32)
-    facts = jnp.pad(jnp.tile(jnp.stack([segment, weight]), (1, 2)), ((0, 6), (0, 0)))
     bf16, f32 = jnp.bfloat16, jnp.float32
     dma = pltpu.SemaphoreType.DMA
+    smem, vmem = pl.BlockSpec(memory_space=pltpu.SMEM), pl.BlockSpec(memory_space=pltpu.VMEM)
     coadd, difference = pl.pallas_call(
         trade_kernel,
-        in_specs=[pl.BlockSpec(memory_space=pltpu.SMEM)] * 2
-        + [pl.BlockSpec(memory_space=pltpu.VMEM)] * 5,
-        out_specs=[pl.BlockSpec(memory_space=pltpu.VMEM)] * 2,
+        in_specs=[smem] * 2 + [vmem] * 5 + [pl.BlockSpec(memory_space=pl.ANY)] * 2,
+        out_specs=[vmem] * 2,
         out_shape=[
-            jax.ShapeDtypeStruct((CELLS * HALF * ROWS, side_len), f32),
+            jax.ShapeDtypeStruct((CELLS * CORES * ROWS, side_len), f32),
             jax.ShapeDtypeStruct((blocks * side_len, side_len), bf16),
         ],
         scratch_shapes=[
-            pltpu.VMEM((STEPS, GROUP, blocks, width), bf16),
+            pltpu.VMEM((blocks, side_len, side_len), bf16),
+            pltpu.VMEM((blocks, side_len, side_len), jnp.int32),
+            pltpu.VMEM((STEPS, ADDERS, blocks, width), bf16),
             pltpu.VMEM((STEPS, GROUP, blocks, width), bf16),
             pltpu.VMEM((STEPS, cells, width), f32),
             pltpu.VMEM((STEPS, cells, width), bf16),
             pltpu.VMEM((STEPS, cells, width), bf16),
             pltpu.VMEM((STEPS, cells, width), bf16),
-            pltpu.VMEM((STEPS, HALF, CELLS, width), bf16),
+            pltpu.VMEM((STEPS, CORES, CELLS, width), bf16),
             pltpu.VMEM((STEPS, GROUP, blocks, width), bf16),
-            pltpu.VMEM((STEPS, GROUP, blocks, width), bf16),
+            pltpu.VMEM((STEPS, ADDERS, blocks, width), bf16),
             pltpu.VMEM((cells, total), bf16),
             pltpu.VMEM((total, cells), bf16),
             pltpu.VMEM((blocks * side_len, side_len), f32),
+            pltpu.VMEM((8, 2 * blocks), f32),
             pltpu.VMEM((GROUP, 8, 2 * blocks), f32),
             pltpu.VMEM((16, total), bf16),
             pltpu.VMEM((8, cells), f32),
             pltpu.VMEM((8, cells), f32),
             pltpu.VMEM((cells, side_len), f32),
-            dma((GROUP,)),
-            dma((GROUP,)),
+            dma((LOADS,)),
+            dma((LOADS,)),
+            dma((STEPS, ADDERS)),
             dma((STEPS, GROUP)),
-            dma((STEPS, GROUP)),
-            dma((GROUP,)),
+            dma((ADDERS,)),
             dma((GROUP,)),
             dma,
             dma,
             dma((STEPS,)),
             dma((STEPS,)),
             dma((STEPS, HALF)),
-            dma((STEPS, HALF)),
+            dma((STEPS, CORES)),
             dma((STEPS, GROUP)),
-            dma((STEPS, GROUP)),
+            dma((STEPS, ADDERS)),
         ],
         compiler_params=pltpu.CompilerParams(
-            collective_id=0, has_side_effects=True, vmem_limit_bytes=56 * 2**20
+            collective_id=0, has_side_effects=True, vmem_limit_bytes=58 * 2**20
         ),
     )(
-        coef_index, coef_table, pixels, mask_bits, facts,
-        jnp.asarray(right_bands, dtype=bf16), jnp.asarray(bands),
+        coef_index, coef_table.T,
+        inv_var.reshape(1, blocks), owner.reshape(1, blocks), cell.reshape(1, blocks),
+        jnp.asarray(right_bands, dtype=bf16), jnp.asarray(bands), pixels, mask_bits,
     )
     return (
-        coadd.reshape(CELLS, HALF * ROWS, side_len),
+        coadd.reshape(CELLS, CORES * ROWS, side_len),
         difference.reshape(blocks, side_len, side_len),
     )
 
@@ -485,7 +552,7 @@
         P(("visit", "patch")),
         P(),
     )
-    fits = mesh.shape["visit"] == GROUP // HALF and mesh.shape["patch"] == 2 * HALF
+    fits = mesh.shape["visit"] * HALF == GROUP and mesh.shape["patch"] == 2 * HALF
     return jax.shard_map(
         row_shards if fits else shards,
         mesh=mesh,

time: 110 us -> 125 us (1.14); the launches traced: 109 us -> 125 us
  Pallas kernels: 101 us -> 121 us
  local copies, waits for them, and re-layouts: 5.82 us -> 3.73 us
  other arithmetic: 1.34 us -> 0 us
    pallas_call x1, Pallas kernels: 101 us -> 121 us  [row_shards(): pl.pallas_call(trade_kernel, in_specs=[smem] * 2 + [vmem] * 5 + [pl.Block...]
    unnamed x5 -> x4, local copies, waits for them, and re-layouts: 5.13 us -> 3.73 us
    another operation x3 -> x0, other arithmetic: 1.34 us -> none  [row_shards(): jnp.stack([segment, weight])]
where the time goes in v3:
time: 125 us
  Pallas kernels  121 us (97%)
  local copies, waits for them, and re-layouts  3.73 us (3%)
    pallas_call x1, Pallas kernels, row_shards(): pl.pallas_call(trade_kernel, in_specs=[smem] * 2 + [vmem] * 5 + [pl.Block...  121 us
    unnamed x4, local copies, waits for them, and re-layouts  3.73 us

profile of v3, /device:TPU:0, one launch (start us, length us, event | category | flops | bytes accessed | tf_op | source)
XLA Modules:
  0.0 125.3 jit_solution(3212056202762595153)
XLA Ops:
  0.6 120.9 %shard_map.104 = (f32[2048,128]{1,0:T(8,128)}, bf16[8192,128]{1,0:T(8,128)(2,1)}) custom-call(s32[64]{0:T(128)} %index_ref.1, f32[9,64]{1,0:T(8,128)} %bitcast.8, f32[1,64]{1,0:T(1,128)} %bitcast.9, s32[1,64]{1,0:T(1,128)} %bitcast.10, s32[1,64]{1,0:T(1,128)} %bitcast.11, bf16[128,768]{1,0:T(8,128)(2,1)} %constant.4.clone.right_ref, ...), custom_call_target="tpu_custom_call" | custom-call | tf_op jit(solution)/shard_map/pallas_call | solution.py:487
  121.5 0.0 copy-start
  121.5 2.4 %copy.13 = f32[64,32,128]{2,1,0:T(8,128)} copy(f32[64,32,128]{2,1,0:T(8,128)} %bitcast.7) | data formatting | bytes 2097152
  123.9 0.0 copy-done
  123.9 1.3 %copy.14 = bf16[64,128,128]{2,1,0:T(8,128)(2,1)} copy(bf16[64,128,128]{2,1,0:T(8,128)(2,1)S(1)} %bitcast.6) | data formatting | bytes 4194304
Async XLA Ops:
  121.5 2.4 %copy-start = (bf16[8192,128]{1,0:T(8,128)(2,1)S(1)}, bf16[8192,128]{1,0:T(8,128)(2,1)}, u32[]{:S(2)}) copy-start(bf16[8192,128]{1,0:T(8,128)(2,1)} %get-tuple-element.5) | copy-start | bytes 6291460

commit v4 on v3

--- a/solution.py
+++ b/solution.py
@@ -149,10 +149,8 @@
     return (coadd_part, difference)
 
 
-GROUP = 16
-HALF = 4
+PLANE = 8
 CORES = 2
-ADDERS = 8
 ROWS = 16
 STEPS = 8
 PAIR = ROWS // STEPS
@@ -178,53 +176,36 @@
 def trade_kernel(
     index_ref, table_ref, inv_var_ref, owner_ref, cell_ref, right_ref, bands_ref, pixels_hbm, mask_hbm,
     coadd_ref, difference_ref,
-    pixels, mask, rows, held, sums, sums_out, sums_in, templates, coadd_in, diffs, diffs_in,
-    weights, picks, wide, facts, facts_in, weight_rows, total_out, total_in, scale,
-    load_pixels, load_mask, send_rows, recv_rows, send_facts, recv_facts, send_total, recv_total,
-    send_sums, recv_sums, send_coadd, recv_coadd, send_diffs, recv_diffs,
+    pixels, mask, rows, held, sums, sums_out, near_in, cross_in, templates, coadd_in, diffs, diffs_in,
+    weights, picks, wide, facts, facts_in, weight_rows, total_out, total_near, total_in, scale,
+    load_pixels, load_mask, send_rows, recv_rows, send_facts, recv_facts,
+    send_total, recv_total_near, recv_total_cross, send_near, recv_near, send_cross, recv_cross,
+    send_back, recv_back, send_coadd, recv_coadd, send_diffs, recv_diffs,
 ):
     blocks, side_len = pixels.shape[0], pixels.shape[1]
-    total = GROUP * blocks
+    total = PLANE * blocks
     cells = weights.shape[0]
     width = PAIR * side_len
     lanes = 2 * blocks
     load = blocks // LOADS
     visit, patch = lax.axis_index("visit"), lax.axis_index("patch")
-    half, place, core = patch // HALF, patch % HALF, patch % CORES
-    me = visit * HALF + place
-    adder = visit * CORES + core
-    adds = patch // CORES == 1 + half
-    skip_self = jnp.where(adds, 1, 0)
+    layer, core = patch // CORES, patch % CORES
+    me = visit * CORES + core
+    inner = (layer + 1) // 2 == 1
+    outer = jnp.logical_not(inner)
+    mate = (visit, (layer + 1 - 2 * (layer % 2)) * CORES + core)
+    across = (visit, (3 - layer) * CORES + core)
+    barrier = pltpu.get_barrier_semaphore()
 
     def device_of(index):
-        return (index // HALF, half * HALF + index % HALF)
-
-    def adder_of(index):
-        return (index // CORES, (1 + half) * CORES + index % CORES)
-
-    partner = (visit, (2 - half) * CORES + core)
-    barrier = pltpu.get_barrier_semaphore()
+        return (index // CORES, layer * CORES + index % CORES)
 
     def peers(act):
         def one(turn, carry):
-            act((me + turn) % GROUP)
+            act((me + turn) % PLANE)
             return carry
 
-        lax.fori_loop(1, GROUP, one, 0)
-
-    def adders(act):
-        def one(turn, carry):
-            act((adder + turn) % ADDERS)
-            return carry
-
-        lax.fori_loop(skip_self, ADDERS, one, 0)
-
-    def places(act):
-        def one(turn, carry):
-            act((place + turn) % HALF)
-            return carry
-
-        lax.fori_loop(1, HALF, one, 0)
+        lax.fori_loop(1, PLANE, one, 0)
 
     def greet(device):
         pl.semaphore_signal(barrier, inc=1, device_id=device, device_id_type=MESH)
@@ -236,60 +217,56 @@
             pltpu.make_async_copy(mask_hbm.at[span], mask.at[span], load_mask.at[part]),
         )
 
-    def facts_copy(target, slot):
+    def send(source, target, send_sem, recv_sem, device):
         return pltpu.make_async_remote_copy(
-            src_ref=facts, dst_ref=facts_in.at[slot],
-            send_sem=send_facts.at[target], recv_sem=recv_facts.at[slot],
-            device_id=adder_of(target), device_id_type=MESH,
-        )
-
-    def rows_copy(step, target, slot):
-        return pltpu.make_async_remote_copy(
-            src_ref=rows.at[step, target], dst_ref=held.at[step, slot],
-            send_sem=send_rows.at[step, target], recv_sem=recv_rows.at[step, slot],
-            device_id=adder_of(target), device_id_type=MESH,
-        )
-
-    def total_copy():
-        return pltpu.make_async_remote_copy(
-            src_ref=total_out, dst_ref=total_in, send_sem=send_total, recv_sem=recv_total,
-            device_id=partner, device_id_type=MESH,
-        )
-
-    def sums_copy(step):
-        return pltpu.make_async_remote_copy(
-            src_ref=sums_out.at[step], dst_ref=sums_in.at[step],
-            send_sem=send_sums.at[step], recv_sem=recv_sums.at[step],
-            device_id=partner, device_id_type=MESH,
-        )
-
-    def coadd_copy(step, peer, slot):
-        start = pl.multiple_of((half * HALF + peer) * CELLS, CELLS)
-        return pltpu.make_async_remote_copy(
-            src_ref=templates.at[step, pl.ds(start, CELLS)], dst_ref=coadd_in.at[step, slot],
-            send_sem=send_coadd.at[step, peer], recv_sem=recv_coadd.at[step, slot],
-            device_id=(visit, half * HALF + peer), device_id_type=MESH,
+            src_ref=source, dst_ref=target, send_sem=send_sem, recv_sem=recv_sem,
+            device_id=device, device_id_type=MESH,
+        )
+
+    def facts_copy(peer, slot):
+        return send(facts, facts_in.at[slot], send_facts.at[peer], recv_facts.at[slot], device_of(peer))
+
+    def rows_copy(step, peer, slot):
+        return send(
+            rows.at[step, peer], held.at[step, slot],
+            send_rows.at[step, peer], recv_rows.at[step, slot], device_of(peer),
+        )
+
+    def total_near_copy():
+        return send(total_out, total_near, send_total, recv_total_near, mate)
+
+    def total_cross_copy():
+        return send(total_out, total_in, send_total, recv_total_cross, across)
+
+    def near_copy(step):
+        return send(sums_out.at[step], near_in.at[step], send_near.at[step], recv_near.at[step], mate)
+
+    def cross_copy(step):
+        return send(sums_out.at[step], cross_in.at[step], send_cross.at[step], recv_cross.at[step], across)
+
+    def back_copy(step):
+        return send(templates.at[step], templates.at[step], send_back.at[step], recv_back.at[step], mate)
+
+    def coadd_copy(step):
+        start = pl.multiple_of((layer * CORES + 1 - core) * CELLS, CELLS)
+        return send(
+            templates.at[step, pl.ds(start, CELLS)], coadd_in.at[step],
+            send_coadd.at[step], recv_coadd.at[step], (visit, layer * CORES + 1 - core),
         )
 
     def diffs_copy(step, peer, slot):
-        return pltpu.make_async_remote_copy(
-            src_ref=diffs.at[step, peer], dst_ref=diffs_in.at[step, slot],
-            send_sem=send_diffs.at[step, peer], recv_sem=recv_diffs.at[step, slot],
-            device_id=device_of(peer), device_id_type=MESH,
+        return send(
+            diffs.at[step, peer], diffs_in.at[step, slot],
+            send_diffs.at[step, peer], recv_diffs.at[step, slot], device_of(peer),
         )
 
     for part in range(LOADS):
         for copy in load_copies(part):
             copy.start()
 
-    @pl.when(adds)
-    def _():
-        peers(lambda peer: greet(device_of(peer)))
-        greet(partner)
-
-    @pl.when(jnp.logical_not(adds))
-    def _():
-        adders(lambda target: greet(adder_of(target)))
+    peers(lambda peer: greet(device_of(peer)))
+    greet(mate)
+    pl.when(inner)(lambda: greet(across))
 
     segment = (owner_ref[...] * CELLS + cell_ref[...]).astype(jnp.float32)
     weight = inv_var_ref[...].astype(jnp.bfloat16).astype(jnp.float32)
@@ -328,92 +305,107 @@
             copy.wait()
         lax.fori_loop(part * load // unit, (part + 1) * load // unit, match_unit, 0)
 
-    pl.semaphore_wait(barrier, jnp.where(adds, GROUP, ADDERS))
-    adders(lambda target: facts_copy(target, me).start())
-
-    def send_step(step, carry):
-        def gather_rows(target, carry):
+    pl.semaphore_wait(barrier, jnp.where(inner, PLANE + 1, PLANE))
+    peers(lambda peer: facts_copy(peer, me).start())
+
+    def send_rows_of(step):
+        def gather_rows(peer, carry):
             for k in range(PAIR):
-                start = target * ROWS + step * PAIR + k
+                start = peer * ROWS + step * PAIR + k
                 values = wide[pl.ds(start, blocks, stride=side_len), :].astype(jnp.bfloat16)
-                rows[step, target, :, k * side_len : (k + 1) * side_len] = values
+                rows[step, peer, :, k * side_len : (k + 1) * side_len] = values
             return carry
 
-        lax.fori_loop(0, ADDERS, gather_rows, 0)
-        adders(lambda target: rows_copy(step, target, me).start())
+        lax.fori_loop(0, PLANE, gather_rows, 0)
+        peers(lambda peer: rows_copy(step, peer, me).start())
+        held[step, pl.ds(me, 1)] = rows[step, pl.ds(me, 1)]
+
+    ahead = 2
+    for step in range(ahead):
+        send_rows_of(step)
+    facts_in[pl.ds(me, 1)] = facts[...].reshape((1,) + facts.shape)
+    peers(lambda peer: facts_copy(peer, peer).wait_recv())
+
+    def make_pickers(pair, carry):
+        first_lanes = lax.broadcasted_iota(jnp.int32, (1, lanes), 1) < blocks
+        segment = jnp.where(first_lanes, facts_in[2 * pair, 0:1, :], facts_in[2 * pair + 1, 0:1, :])
+        weight = jnp.where(first_lanes, facts_in[2 * pair, 1:2, :], facts_in[2 * pair + 1, 1:2, :])
+        start = pl.multiple_of(pair * lanes, lanes)
+        cell = lax.broadcasted_iota(jnp.int32, (cells, lanes), 0).astype(jnp.float32)
+        weights[:, pl.ds(start, lanes)] = jnp.where(cell == segment, weight, 0.0).astype(jnp.bfloat16)
+        weight_rows[:, pl.ds(start, lanes)] = jnp.broadcast_to(weight, (16, lanes)).astype(jnp.bfloat16)
+        segment_column = jnp.broadcast_to(segment, (lanes, lanes)).T
+        for c in range(cells // lanes):
+            cell = lax.broadcasted_iota(jnp.int32, (lanes, lanes), 1) + c * lanes
+            chosen = jnp.where(cell.astype(jnp.float32) == segment_column, 1.0, 0.0)
+            picks[pl.ds(start, lanes), c * lanes : (c + 1) * lanes] = chosen.astype(jnp.bfloat16)
         return carry
 
-    lax.fori_loop(0, STEPS, send_step, 0)
-
-    @pl.when(adds)
-    def _():
-        def keep_own(step, carry):
-            held[step, pl.ds(me, 1)] = rows[step, pl.ds(adder, 1)]
-            return carry
-
-        lax.fori_loop(0, STEPS, keep_own, 0)
-        facts_in[pl.ds(me, 1)] = facts[...].reshape((1,) + facts.shape)
-        peers(lambda peer: facts_copy(adder, peer).wait_recv())
-
-        def make_pickers(pair, carry):
-            first_lanes = lax.broadcasted_iota(jnp.int32, (1, lanes), 1) < blocks
-            segment = jnp.where(first_lanes, facts_in[2 * pair, 0:1, :], facts_in[2 * pair + 1, 0:1, :])
-            weight = jnp.where(first_lanes, facts_in[2 * pair, 1:2, :], facts_in[2 * pair + 1, 1:2, :])
-            start = pl.multiple_of(pair * lanes, lanes)
-            cell = lax.broadcasted_iota(jnp.int32, (cells, lanes), 0).astype(jnp.float32)
-            weights[:, pl.ds(start, lanes)] = jnp.where(cell == segment, weight, 0.0).astype(jnp.bfloat16)
-            weight_rows[:, pl.ds(start, lanes)] = jnp.broadcast_to(weight, (16, lanes)).astype(jnp.bfloat16)
-            segment_column = jnp.broadcast_to(segment, (lanes, lanes)).T
-            for c in range(cells // lanes):
-                cell = lax.broadcasted_iota(jnp.int32, (lanes, lanes), 1) + c * lanes
-                chosen = jnp.where(cell.astype(jnp.float32) == segment_column, 1.0, 0.0)
-                picks[pl.ds(start, lanes), c * lanes : (c + 1) * lanes] = chosen.astype(jnp.bfloat16)
-            return carry
-
-        lax.fori_loop(0, GROUP // 2, make_pickers, 0)
-        part_total = jnp.dot(weight_rows[...], picks[...], preferred_element_type=jnp.float32)
-        total_out[...] = part_total[0:8]
-        total_copy().start()
+    lax.fori_loop(0, PLANE // 2, make_pickers, 0)
+    part_total = jnp.dot(weight_rows[...], picks[...], preferred_element_type=jnp.float32)
+    total_out[...] = part_total[0:8]
+    pl.when(outer)(lambda: total_near_copy().start())
 
     def add_up(step):
-        peers(lambda peer: rows_copy(step, adder, peer).wait_recv())
+        peers(lambda peer: rows_copy(step, peer, peer).wait_recv())
         flat = held[step].reshape(total, width)
         part_sum = jnp.dot(weights[...], flat, preferred_element_type=jnp.float32)
-        sums[step] = part_sum
-        sums_out[step] = part_sum.astype(jnp.bfloat16)
-        sums_copy(step).start()
+
+        @pl.when(inner)
+        def _():
+            sums[step] = part_sum
+
+        @pl.when(outer)
+        def _():
+            sums_out[step] = part_sum.astype(jnp.bfloat16)
+            near_copy(step).start()
+
+    def join_totals():
+        total_near_copy().wait_recv()
+        total_out[...] += total_near[...]
+        total_cross_copy().start()
+
+    def join(step):
+        near_copy(step).wait_recv()
+        joint = sums[step] + near_in[step].astype(jnp.float32)
+        sums[step] = joint
+        sums_out[step] = joint.astype(jnp.bfloat16)
+        cross_copy(step).start()
 
     def get_scale():
-        total_copy().wait_recv()
+        total_cross_copy().wait_recv()
         scale_row = 1.0 / jnp.maximum(total_out[0:1] + total_in[0:1], 1.0)
         for c in range(cells // lanes):
             scale[c * lanes : (c + 1) * lanes] = jnp.broadcast_to(
                 scale_row[:, c * lanes : (c + 1) * lanes], (lanes, lanes)
             ).T
 
-    def take_off(step):
-        sums_copy(step).wait_recv()
-        whole_sum = sums[step] + sums_in[step].astype(jnp.float32)
+    def settle(step):
+        cross_copy(step).wait_recv()
+        whole_sum = sums[step] + cross_in[step].astype(jnp.float32)
         for k in range(PAIR):
             lane = slice(k * side_len, (k + 1) * side_len)
             templates[step, :, lane] = (whole_sum[:, lane] * scale[...]).astype(jnp.bfloat16)
+        back_copy(step).start()
+
+    def take_off(step):
         flat = held[step].reshape(total, width)
         chosen = jnp.dot(picks[...], templates[step], preferred_element_type=jnp.float32)
         change = (flat.astype(jnp.float32) - chosen).astype(jnp.bfloat16)
-        diffs[step] = change.reshape(GROUP, blocks, width)
-        peers(lambda peer: diffs_copy(step, peer, adder).start())
-        places(lambda peer: coadd_copy(step, peer, core).start())
+        diffs[step] = change.reshape(PLANE, blocks, width)
+        peers(lambda peer: diffs_copy(step, peer, me).start())
+        coadd_copy(step).start()
+        diffs_in[step, pl.ds(me, 1)] = diffs[step, pl.ds(me, 1)]
+
+    rows_here = CORES * ROWS
+
+    def finish(step):
         start = pl.multiple_of(patch * CELLS, CELLS)
-        coadd_in[step, pl.ds(core, 1)] = templates[step, pl.ds(start, CELLS)].reshape(1, CELLS, width)
-        diffs_in[step, pl.ds(adder, 1)] = diffs[step, pl.ds(me, 1)]
-
-    rows_here = CORES * ROWS
-
-    def wait_coadd(step, source):
-        coadd_copy(step, place, source).wait_recv()
-
-    def finish(step):
-        adders(lambda source: diffs_copy(step, me, source).wait_recv())
+        own = templates[step, pl.ds(start, CELLS)].astype(jnp.float32)
+        for k in range(PAIR):
+            row = core * ROWS + step * PAIR + k
+            coadd_ref[pl.ds(row, CELLS, stride=rows_here), :] = own[:, k * side_len : (k + 1) * side_len]
+        peers(lambda peer: diffs_copy(step, peer, peer).wait_recv())
 
         def spread(source, carry):
             values = diffs_in[step, source].astype(jnp.float32)
@@ -424,27 +416,35 @@
                 ]
             return carry
 
-        lax.fori_loop(0, ADDERS, spread, 0)
-        wait_coadd(step, 1 - core)
-        pl.when(jnp.logical_not(adds))(lambda: wait_coadd(step, core))
-        for source in range(CORES):
-            values = coadd_in[step, source].astype(jnp.float32)
-            for k in range(PAIR):
-                row = source * ROWS + step * PAIR + k
-                coadd_ref[pl.ds(row, CELLS, stride=rows_here), :] = values[
-                    :, k * side_len : (k + 1) * side_len
-                ]
-
-    lag = 2
+        lax.fori_loop(0, PLANE, spread, 0)
+        coadd_copy(step).wait_recv()
+        other = coadd_in[step].astype(jnp.float32)
+        for k in range(PAIR):
+            row = (1 - core) * ROWS + step * PAIR + k
+            coadd_ref[pl.ds(row, CELLS, stride=rows_here), :] = other[:, k * side_len : (k + 1) * side_len]
 
     def one_step(step, carry):
-        pl.when(adds & (step < STEPS))(lambda: add_up(step))
-        pl.when(adds & (step == 1))(get_scale)
-        pl.when(adds & (step >= 1) & (step <= STEPS))(lambda: take_off(step - 1))
-        pl.when(step >= lag)(lambda: finish(step - lag))
+        pl.when(step < STEPS)(lambda: add_up(step))
+        pl.when(step + ahead < STEPS)(lambda: send_rows_of(step + ahead))
+
+        @pl.when(inner)
+        def _():
+            pl.when(step == 1)(join_totals)
+            pl.when((step >= 1) & (step <= STEPS))(lambda: join(step - 1))
+            pl.when(step == 2)(get_scale)
+            pl.when((step >= 2) & (step <= STEPS + 1))(lambda: settle(step - 2))
+
+        late = jnp.where(inner, 2, 3)
+
+        @pl.when((step >= late) & (step < STEPS + late))
+        def _():
+            pl.when(outer)(lambda: back_copy(step - late).wait_recv())
+            take_off(step - late)
+
+        pl.when(step >= 4)(lambda: finish(step - 4))
         return carry
 
-    lax.fori_loop(0, STEPS + lag, one_step, 0)
+    lax.fori_loop(0, STEPS + 4, one_step, 0)
 
     def narrow(part, carry):
         start = pl.multiple_of(part * 512, 512)
@@ -453,31 +453,30 @@
 
     lax.fori_loop(0, wide.shape[0] // 512, narrow, 0)
 
-    adders(lambda target: facts_copy(target, me).wait_send())
-
-    def sent_rows(step, carry):
-        adders(lambda target: rows_copy(step, target, me).wait_send())
+    peers(lambda peer: facts_copy(peer, me).wait_send())
+    pl.when(inner)(lambda: total_cross_copy().wait_send())
+    pl.when(outer)(lambda: total_near_copy().wait_send())
+
+    def sent(step, carry):
+        peers(lambda peer: rows_copy(step, peer, me).wait_send())
+        peers(lambda peer: diffs_copy(step, peer, me).wait_send())
+        coadd_copy(step).wait_send()
+
+        @pl.when(inner)
+        def _():
+            cross_copy(step).wait_send()
+            back_copy(step).wait_send()
+
+        pl.when(outer)(lambda: near_copy(step).wait_send())
         return carry
 
-    lax.fori_loop(0, STEPS, sent_rows, 0)
-
-    @pl.when(adds)
-    def _():
-        total_copy().wait_send()
-
-        def sent(step, carry):
-            sums_copy(step).wait_send()
-            peers(lambda peer: diffs_copy(step, peer, adder).wait_send())
-            places(lambda peer: coadd_copy(step, peer, core).wait_send())
-            return carry
-
-        lax.fori_loop(0, STEPS, sent, 0)
+    lax.fori_loop(0, STEPS, sent, 0)
 
 
 def row_shards(pixels, mask_bits, inv_var, owner, cell, coef_index, coef_table):
     blocks, side_len = pixels.shape[0], pixels.shape[1]
     cells = lax.axis_size("patch") * CELLS
-    total = GROUP * blocks
+    total = PLANE * blocks
     width = PAIR * side_len
     bands = fixed_bands(side_len)
     right_bands = np.transpose(bands, (2, 0, 1)).reshape(side_len, 6 * side_len)
@@ -495,39 +494,38 @@
         scratch_shapes=[
             pltpu.VMEM((blocks, side_len, side_len), bf16),
             pltpu.VMEM((blocks, side_len, side_len), jnp.int32),
-            pltpu.VMEM((STEPS, ADDERS, blocks, width), bf16),
-            pltpu.VMEM((STEPS, GROUP, blocks, width), bf16),
+            pltpu.VMEM((STEPS, PLANE, blocks, width), bf16),
+            pltpu.VMEM((STEPS, PLANE, blocks, width), bf16),
             pltpu.VMEM((STEPS, cells, width), f32),
             pltpu.VMEM((STEPS, cells, width), bf16),
             pltpu.VMEM((STEPS, cells, width), bf16),
             pltpu.VMEM((STEPS, cells, width), bf16),
-            pltpu.VMEM((STEPS, CORES, CELLS, width), bf16),
-            pltpu.VMEM((STEPS, GROUP, blocks, width), bf16),
-            pltpu.VMEM((STEPS, ADDERS, blocks, width), bf16),
+            pltpu.VMEM((STEPS, cells, width), bf16),
+            pltpu.VMEM((STEPS, CELLS, width), bf16),
+            pltpu.VMEM((STEPS, PLANE, blocks, width), bf16),
+            pltpu.VMEM((STEPS, PLANE, blocks, width), bf16),
             pltpu.VMEM((cells, total), bf16),
             pltpu.VMEM((total, cells), bf16),
             pltpu.VMEM((blocks * side_len, side_len), f32),
             pltpu.VMEM((8, 2 * blocks), f32),
-            pltpu.VMEM((GROUP, 8, 2 * blocks), f32),
+            pltpu.VMEM((PLANE, 8, 2 * blocks), f32),
             pltpu.VMEM((16, total), bf16),
+            pltpu.VMEM((8, cells), f32),
             pltpu.VMEM((8, cells), f32),
             pltpu.VMEM((8, cells), f32),
             pltpu.VMEM((cells, side_len), f32),
             dma((LOADS,)),
             dma((LOADS,)),
-            dma((STEPS, ADDERS)),
-            dma((STEPS, GROUP)),
-            dma((ADDERS,)),
-            dma((GROUP,)),
+            dma((STEPS, PLANE)),
+            dma((STEPS, PLANE)),
+            dma((PLANE,)),
+            dma((PLANE,)),
             dma,
             dma,
-            dma((STEPS,)),
-            dma((STEPS,)),
-            dma((STEPS, HALF)),
-            dma((STEPS, CORES)),
-            dma((STEPS, GROUP)),
-            dma((STEPS, ADDERS)),
-        ],
+            dma,
+        ]
+        + [dma((STEPS,))] * 8
+        + [dma((STEPS, PLANE))] * 2,
         compiler_params=pltpu.CompilerParams(
             collective_id=0, has_side_effects=True, vmem_limit_bytes=58 * 2**20
         ),
@@ -552,7 +550,7 @@
         P(("visit", "patch")),
         P(),
     )
-    fits = mesh.shape["visit"] * HALF == GROUP and mesh.shape["patch"] == 2 * HALF
+    fits = mesh.shape["visit"] * CORES == PLANE and mesh.shape["patch"] == 4 * CORES
     return jax.shard_map(
         row_shards if fits else shards,
         mesh=mesh,

time: 125 us -> 101 us (0.81)
  Pallas kernels: 121 us -> 96.6 us
    pallas_call x1, Pallas kernels: 121 us -> 96.6 us  [row_shards(): pl.pallas_call(trade_kernel, in_specs=[smem] * 2 + [vmem] * 5 + [pl.Block...]
where the time goes in v4:
time: 101 us
  Pallas kernels  96.6 us (96%)
  local copies, waits for them, and re-layouts  3.73 us (4%)
    pallas_call x1, Pallas kernels, row_shards(): pl.pallas_call(trade_kernel, in_specs=[smem] * 2 + [vmem] * 5 + [pl.Block...  96.6 us
    unnamed x4, local copies, waits for them, and re-layouts  3.73 us

profile of v4, /device:TPU:0, one launch (start us, length us, event | category | flops | bytes accessed | tf_op | source)
XLA Modules:
  0.0 101.0 jit_solution(788835833145408043)
XLA Ops:
  0.6 96.6 %shard_map.104 = (f32[2048,128]{1,0:T(8,128)}, bf16[8192,128]{1,0:T(8,128)(2,1)}) custom-call(s32[64]{0:T(128)} %index_ref.1, f32[9,64]{1,0:T(8,128)} %bitcast.8, f32[1,64]{1,0:T(1,128)} %bitcast.9, s32[1,64]{1,0:T(1,128)} %bitcast.10, s32[1,64]{1,0:T(1,128)} %bitcast.11, bf16[128,768]{1,0:T(8,128)(2,1)} %constant.4.clone.right_ref, ...), custom_call_target="tpu_custom_call" | custom-call | tf_op jit(solution)/shard_map/pallas_call | solution.py:486
  97.3 0.0 copy-start
  97.3 2.4 %copy.13 = f32[64,32,128]{2,1,0:T(8,128)} copy(f32[64,32,128]{2,1,0:T(8,128)} %bitcast.7) | data formatting | bytes 2097152
  99.7 0.0 copy-done
  99.7 1.3 %copy.14 = bf16[64,128,128]{2,1,0:T(8,128)(2,1)} copy(bf16[64,128,128]{2,1,0:T(8,128)(2,1)S(1)} %bitcast.6) | data formatting | bytes 4194304
Async XLA Ops:
  97.3 2.4 %copy-start = (bf16[8192,128]{1,0:T(8,128)(2,1)S(1)}, bf16[8192,128]{1,0:T(8,128)(2,1)}, u32[]{:S(2)}) copy-start(bf16[8192,128]{1,0:T(8,128)(2,1)} %get-tuple-element.5) | copy-start | bytes 6291460

commit v5 on v4

--- a/solution.py
+++ b/solution.py
@@ -155,6 +155,7 @@
 STEPS = 8
 PAIR = ROWS // STEPS
 LOADS = 4
+PARTS = 4
 MESH = pl.DeviceIdType.MESH
 
 
@@ -238,14 +239,38 @@
     def total_cross_copy():
         return send(total_out, total_in, send_total, recv_total_cross, across)
 
-    def near_copy(step):
-        return send(sums_out.at[step], near_in.at[step], send_near.at[step], recv_near.at[step], mate)
-
-    def cross_copy(step):
-        return send(sums_out.at[step], cross_in.at[step], send_cross.at[step], recv_cross.at[step], across)
-
-    def back_copy(step):
-        return send(templates.at[step], templates.at[step], send_back.at[step], recv_back.at[step], mate)
+    some = cells // PARTS
+
+    def cells_of(part):
+        return pl.ds(pl.multiple_of(part * some, some), some)
+
+    def every_part(act):
+        def one(part, carry):
+            act(part)
+            return carry
+
+        lax.fori_loop(0, PARTS, one, 0)
+
+    def near_copy(step, part):
+        span = cells_of(part)
+        return send(
+            sums_out.at[step, span], near_in.at[step, span],
+            send_near.at[step, part], recv_near.at[step, part], mate,
+        )
+
+    def cross_copy(step, part):
+        span = cells_of(part)
+        return send(
+            sums_out.at[step, span], cross_in.at[step, span],
+            send_cross.at[step, part], recv_cross.at[step, part], across,
+        )
+
+    def back_copy(step, part):
+        span = cells_of(part)
+        return send(
+            templates.at[step, span], templates.at[step, span],
+            send_back.at[step, part], recv_back.at[step, part], mate,
+        )
 
     def coadd_copy(step):
         start = pl.multiple_of((layer * CORES + 1 - core) * CELLS, CELLS)
@@ -358,19 +383,20 @@
         @pl.when(outer)
         def _():
             sums_out[step] = part_sum.astype(jnp.bfloat16)
-            near_copy(step).start()
+            every_part(lambda part: near_copy(step, part).start())
 
     def join_totals():
         total_near_copy().wait_recv()
         total_out[...] += total_near[...]
         total_cross_copy().start()
 
-    def join(step):
-        near_copy(step).wait_recv()
-        joint = sums[step] + near_in[step].astype(jnp.float32)
-        sums[step] = joint
-        sums_out[step] = joint.astype(jnp.bfloat16)
-        cross_copy(step).start()
+    def join(step, part):
+        near_copy(step, part).wait_recv()
+        span = cells_of(part)
+        joint = sums[step, span] + near_in[step, span].astype(jnp.float32)
+        sums[step, span] = joint
+        sums_out[step, span] = joint.astype(jnp.bfloat16)
+        cross_copy(step, part).start()
 
     def get_scale():
         total_cross_copy().wait_recv()
@@ -380,13 +406,14 @@
                 scale_row[:, c * lanes : (c + 1) * lanes], (lanes, lanes)
             ).T
 
-    def settle(step):
-        cross_copy(step).wait_recv()
-        whole_sum = sums[step] + cross_in[step].astype(jnp.float32)
+    def settle(step, part):
+        cross_copy(step, part).wait_recv()
+        span = cells_of(part)
+        whole_sum = sums[step, span] + cross_in[step, span].astype(jnp.float32)
         for k in range(PAIR):
             lane = slice(k * side_len, (k + 1) * side_len)
-            templates[step, :, lane] = (whole_sum[:, lane] * scale[...]).astype(jnp.bfloat16)
-        back_copy(step).start()
+            templates[step, span, lane] = (whole_sum[:, lane] * scale[span]).astype(jnp.bfloat16)
+        back_copy(step, part).start()
 
     def take_off(step):
         flat = held[step].reshape(total, width)
@@ -430,21 +457,22 @@
         @pl.when(inner)
         def _():
             pl.when(step == 1)(join_totals)
-            pl.when((step >= 1) & (step <= STEPS))(lambda: join(step - 1))
+            pl.when((step >= 1) & (step <= STEPS))(lambda: every_part(lambda part: join(step - 1, part)))
             pl.when(step == 2)(get_scale)
-            pl.when((step >= 2) & (step <= STEPS + 1))(lambda: settle(step - 2))
-
-        late = jnp.where(inner, 2, 3)
+            pl.when((step >= 2) & (step <= STEPS + 1))(lambda: every_part(lambda part: settle(step - 2, part)))
+
+        late = jnp.where(inner, 2, 6)
 
         @pl.when((step >= late) & (step < STEPS + late))
         def _():
-            pl.when(outer)(lambda: back_copy(step - late).wait_recv())
+            pl.when(outer)(lambda: every_part(lambda part: back_copy(step - late, part).wait_recv()))
             take_off(step - late)
 
-        pl.when(step >= 4)(lambda: finish(step - 4))
+        last = late + 1
+        pl.when((step >= last) & (step < STEPS + last))(lambda: finish(step - last))
         return carry
 
-    lax.fori_loop(0, STEPS + 4, one_step, 0)
+    lax.fori_loop(0, jnp.where(inner, STEPS + 3, STEPS + 7), one_step, 0)
 
     def narrow(part, carry):
         start = pl.multiple_of(part * 512, 512)
@@ -464,10 +492,10 @@
 
         @pl.when(inner)
         def _():
-            cross_copy(step).wait_send()
-            back_copy(step).wait_send()
-
-        pl.when(outer)(lambda: near_copy(step).wait_send())
+            every_part(lambda part: cross_copy(step, part).wait_send())
+            every_part(lambda part: back_copy(step, part).wait_send())
+
+        pl.when(outer)(lambda: every_part(lambda part: near_copy(step, part).wait_send()))
         return carry
 
     lax.fori_loop(0, STEPS, sent, 0)
@@ -524,7 +552,8 @@
             dma,
             dma,
         ]
-        + [dma((STEPS,))] * 8
+        + [dma((STEPS, PARTS))] * 6
+        + [dma((STEPS,))] * 2
         + [dma((STEPS, PLANE))] * 2,
         compiler_params=pltpu.CompilerParams(
             collective_id=0, has_side_effects=True, vmem_limit_bytes=58 * 2**20

time: 101 us -> 99.7 us (0.987)
  Pallas kernels: 96.6 us -> 95.1 us
    pallas_call x1, Pallas kernels: 96.6 us -> 95.1 us  [row_shards(): pl.pallas_call(trade_kernel, in_specs=[smem] * 2 + [vmem] * 5 + [pl.Block...]
where the time goes in v5:
time: 99.7 us; the launch traced here: 99.5 us
  Pallas kernels  95.1 us (95%)
  local copies, waits for them, and re-layouts  3.73 us (4%)
    pallas_call x1, Pallas kernels, row_shards(): pl.pallas_call(trade_kernel, in_specs=[smem] * 2 + [vmem] * 5 + [pl.Block...  95.1 us
    unnamed x4, local copies, waits for them, and re-layouts  3.73 us

profile of v5, /device:TPU:0, one launch (start us, length us, event | category | flops | bytes accessed | tf_op | source)
XLA Modules:
  0.0 99.5 jit_solution(2975929318945886478)
XLA Ops:
  0.6 95.1 %shard_map.104 = (f32[2048,128]{1,0:T(8,128)}, bf16[8192,128]{1,0:T(8,128)(2,1)}) custom-call(s32[64]{0:T(128)} %index_ref.1, f32[9,64]{1,0:T(8,128)} %bitcast.8, f32[1,64]{1,0:T(1,128)} %bitcast.9, s32[1,64]{1,0:T(1,128)} %bitcast.10, s32[1,64]{1,0:T(1,128)} %bitcast.11, bf16[128,768]{1,0:T(8,128)(2,1)} %constant.4.clone.right_ref, ...), custom_call_target="tpu_custom_call" | custom-call | tf_op jit(solution)/shard_map/pallas_call | solution.py:514
  95.8 0.0 copy-start
  95.8 2.4 %copy.13 = f32[64,32,128]{2,1,0:T(8,128)} copy(f32[64,32,128]{2,1,0:T(8,128)} %bitcast.7) | data formatting | bytes 2097152
  98.2 0.0 copy-done
  98.2 1.3 %copy.14 = bf16[64,128,128]{2,1,0:T(8,128)(2,1)} copy(bf16[64,128,128]{2,1,0:T(8,128)(2,1)S(1)} %bitcast.6) | data formatting | bytes 4194304
Async XLA Ops:
  95.8 2.4 %copy-start = (bf16[8192,128]{1,0:T(8,128)(2,1)S(1)}, bf16[8192,128]{1,0:T(8,128)(2,1)}, u32[]{:S(2)}) copy-start(bf16[8192,128]{1,0:T(8,128)(2,1)} %get-tuple-element.5) | copy-start | bytes 6291460

commit v6 on v5

--- a/solution.py
+++ b/solution.py
@@ -152,7 +152,7 @@
 PLANE = 8
 CORES = 2
 ROWS = 16
-STEPS = 8
+STEPS = 4
 PAIR = ROWS // STEPS
 LOADS = 4
 PARTS = 4
@@ -451,9 +451,6 @@
             coadd_ref[pl.ds(row, CELLS, stride=rows_here), :] = other[:, k * side_len : (k + 1) * side_len]
 
     def one_step(step, carry):
-        pl.when(step < STEPS)(lambda: add_up(step))
-        pl.when(step + ahead < STEPS)(lambda: send_rows_of(step + ahead))
-
         @pl.when(inner)
         def _():
             pl.when(step == 1)(join_totals)
@@ -461,7 +458,10 @@
             pl.when(step == 2)(get_scale)
             pl.when((step >= 2) & (step <= STEPS + 1))(lambda: every_part(lambda part: settle(step - 2, part)))
 
-        late = jnp.where(inner, 2, 6)
+        pl.when(step < STEPS)(lambda: add_up(step))
+        pl.when(step + ahead < STEPS)(lambda: send_rows_of(step + ahead))
+
+        late = jnp.where(inner, 2, 4)
 
         @pl.when((step >= late) & (step < STEPS + late))
         def _():
@@ -472,7 +472,7 @@
         pl.when((step >= last) & (step < STEPS + last))(lambda: finish(step - last))
         return carry
 
-    lax.fori_loop(0, jnp.where(inner, STEPS + 3, STEPS + 7), one_step, 0)
+    lax.fori_loop(0, jnp.where(inner, STEPS + 3, STEPS + 5), one_step, 0)
 
     def narrow(part, carry):
         start = pl.multiple_of(part * 512, 512)

time: 99.7 us -> 114 us (1.14)
  Pallas kernels: 95.1 us -> 109 us
    pallas_call x1, Pallas kernels: 95.1 us -> 109 us  [row_shards(): pl.pallas_call(trade_kernel, in_specs=[smem] * 2 + [vmem] * 5 + [pl.Block...]
where the time goes in v6:
time: 114 us
  Pallas kernels  109 us (96%)
  local copies, waits for them, and re-layouts  3.73 us (3%)
    pallas_call x1, Pallas kernels, row_shards(): pl.pallas_call(trade_kernel, in_specs=[smem] * 2 + [vmem] * 5 + [pl.Block...  109 us
    unnamed x4, local copies, waits for them, and re-layouts  3.73 us

profile of v6, /device:TPU:0, one launch (start us, length us, event | category | flops | bytes accessed | tf_op | source)
XLA Modules:
  0.0 113.5 jit_solution(5379003692803435846)
XLA Ops:
  0.6 109.2 %shard_map.104 = (f32[2048,128]{1,0:T(8,128)}, bf16[8192,128]{1,0:T(8,128)(2,1)}) custom-call(s32[64]{0:T(128)} %index_ref.1, f32[9,64]{1,0:T(8,128)} %bitcast.8, f32[1,64]{1,0:T(1,128)} %bitcast.9, s32[1,64]{1,0:T(1,128)} %bitcast.10, s32[1,64]{1,0:T(1,128)} %bitcast.11, bf16[128,768]{1,0:T(8,128)(2,1)} %constant.4.clone.right_ref, ...), custom_call_target="tpu_custom_call" | custom-call | tf_op jit(solution)/shard_map/pallas_call | solution.py:514
  109.8 0.0 copy-start
  109.8 2.4 %copy.13 = f32[64,32,128]{2,1,0:T(8,128)} copy(f32[64,32,128]{2,1,0:T(8,128)} %bitcast.7) | data formatting | bytes 2097152
  112.2 0.0 copy-done
  112.2 1.3 %copy.14 = bf16[64,128,128]{2,1,0:T(8,128)(2,1)} copy(bf16[64,128,128]{2,1,0:T(8,128)(2,1)S(1)} %bitcast.6) | data formatting | bytes 4194304
Async XLA Ops:
  109.8 2.4 %copy-start = (bf16[8192,128]{1,0:T(8,128)(2,1)S(1)}, bf16[8192,128]{1,0:T(8,128)(2,1)}, u32[]{:S(2)}) copy-start(bf16[8192,128]{1,0:T(8,128)(2,1)} %get-tuple-element.5) | copy-start | bytes 6291460

commit v7 on v6

--- a/solution.py
+++ b/solution.py
@@ -152,10 +152,10 @@
 PLANE = 8
 CORES = 2
 ROWS = 16
-STEPS = 4
+STEPS = 16
 PAIR = ROWS // STEPS
 LOADS = 4
-PARTS = 4
+PARTS = 2
 MESH = pl.DeviceIdType.MESH
 
 
@@ -461,7 +461,7 @@
         pl.when(step < STEPS)(lambda: add_up(step))
         pl.when(step + ahead < STEPS)(lambda: send_rows_of(step + ahead))
 
-        late = jnp.where(inner, 2, 4)
+        late = jnp.where(inner, 2, 7)
 
         @pl.when((step >= late) & (step < STEPS + late))
         def _():
@@ -472,7 +472,7 @@
         pl.when((step >= last) & (step < STEPS + last))(lambda: finish(step - last))
         return carry
 
-    lax.fori_loop(0, jnp.where(inner, STEPS + 3, STEPS + 5), one_step, 0)
+    lax.fori_loop(0, jnp.where(inner, STEPS + 3, STEPS + 8), one_step, 0)
 
     def narrow(part, carry):
         start = pl.multiple_of(part * 512, 512)

time: 114 us -> 106 us (0.930)
  Pallas kernels: 109 us -> 102 us
    pallas_call x1, Pallas kernels: 109 us -> 102 us  [row_shards(): pl.pallas_call(trade_kernel, in_specs=[smem] * 2 + [vmem] * 5 + [pl.Block...]
where the time goes in v7:
time: 106 us
  Pallas kernels  102 us (96%)
  local copies, waits for them, and re-layouts  3.73 us (4%)
    pallas_call x1, Pallas kernels, row_shards(): pl.pallas_call(trade_kernel, in_specs=[smem] * 2 + [vmem] * 5 + [pl.Block...  102 us
    unnamed x4, local copies, waits for them, and re-layouts  3.73 us

profile of v7, /device:TPU:0, one launch (start us, length us, event | category | flops | bytes accessed | tf_op | source)
XLA Modules:
  0.0 106.1 jit_solution(2220757155768889535)
XLA Ops:
  0.6 101.7 %shard_map.104 = (f32[2048,128]{1,0:T(8,128)}, bf16[8192,128]{1,0:T(8,128)(2,1)}) custom-call(s32[64]{0:T(128)} %index_ref.1, f32[9,64]{1,0:T(8,128)} %bitcast.8, f32[1,64]{1,0:T(1,128)} %bitcast.9, s32[1,64]{1,0:T(1,128)} %bitcast.10, s32[1,64]{1,0:T(1,128)} %bitcast.11, bf16[128,768]{1,0:T(8,128)(2,1)} %constant.4.clone.right_ref, ...), custom_call_target="tpu_custom_call" | custom-call | tf_op jit(solution)/shard_map/pallas_call | solution.py:514
  102.3 0.0 copy-start
  102.4 2.4 %copy.13 = f32[64,32,128]{2,1,0:T(8,128)} copy(f32[64,32,128]{2,1,0:T(8,128)} %bitcast.7) | data formatting | bytes 2097152
  104.8 0.0 copy-done
  104.8 1.3 %copy.14 = bf16[64,128,128]{2,1,0:T(8,128)(2,1)} copy(bf16[64,128,128]{2,1,0:T(8,128)(2,1)S(1)} %bitcast.6) | data formatting | bytes 4194304
Async XLA Ops:
  102.3 2.4 %copy-start = (bf16[8192,128]{1,0:T(8,128)(2,1)S(1)}, bf16[8192,128]{1,0:T(8,128)(2,1)}, u32[]{:S(2)}) copy-start(bf16[8192,128]{1,0:T(8,128)(2,1)} %get-tuple-element.5) | copy-start | bytes 6291460
